TPU v7x, 256 devices: a whole 4x4x8 slice. The times are simulated.
256 devices in a mesh: dp: 4 (over y), expert: 8 (over z), etp: 8 (over x, core).
Axes of the slice: x: 4, y: 4, z: 8, core: 2. Of those that a mesh axis runs over, the one named last changes fastest.
Arguments:
- tokens: bfloat16 [4096, 3072], P(('dp', 'expert')), may hold values from -6 to 6
- grad_out: bfloat16 [4096, 3072], P(('dp', 'expert')), may hold values from -6 to 6
- gate_prob: float32 [4096, 2], P(('dp', 'expert')), may hold values from 0.1 to 1
- expert_ids: int32 [4096, 2], P(('dp', 'expert')), may hold values from 0 to 7, all different within a row; in each aligned block of 128 rows (0 to 127, 128 to 255, ...) at most 36 rows name the same one
- w_gate: bfloat16 [8, 3072, 8192], P('expert', None, ('dp', 'etp')), may hold values from -0.109375 to 0.109375
- w_up: bfloat16 [8, 3072, 8192], P('expert', None, ('dp', 'etp')), may hold values from -0.109375 to 0.109375
- w_down: bfloat16 [8, 8192, 3072], P('expert', ('dp', 'etp')), may hold values from -0.0625 to 0.0625
Outputs:
- grad_tokens: bfloat16 [4096, 3072], P(('dp', 'expert'), 'etp')
- grad_w_gate: bfloat16 [8, 3072, 8192], P('expert', None, ('dp', 'etp'))
- grad_w_up: bfloat16 [8, 3072, 8192], P('expert', None, ('dp', 'etp'))
- grad_w_down: bfloat16 [8, 8192, 3072], P('expert', ('dp', 'etp'))
Inputs may be any that keep to these rules, and one draw needn't show every extreme that they name: `expert_ids`: each row names two different experts. Within each aligned block of 128 rows no expert is named by more than 36 rows, a bound that some block reaches.
All inputs are finite; a program needn't handle non-finite values.
Results may differ from a plain program's by a relative error of at most 0.02.
Values may be sent and summed in bfloat16 or wider, within the bound.
No kernel may reach another device: no remote copies, remote signals or barrier semaphores. Data moves between devices by JAX's collectives and lax.ppermute only.
A program may use at most 128 MiB of HBM per device.

v0:
```python
import jax
import jax.numpy as jnp
from jax import lax
from jax.experimental import pallas as pl
from jax.experimental.pallas import tpu as pltpu
from jax.sharding import Mesh, PartitionSpec as P

BF = jnp.bfloat16
F32 = jnp.float32
INSIDE = pl.BlockSpec(memory_space=pltpu.VMEM)
SCALARS = pl.BlockSpec(memory_space=pltpu.SMEM)


def swap(a):
    return lax.ppermute(a, "core", [(0, 1), (1, 0)])


def ring(a, second, step):
    nd, nx = lax.axis_size("dp"), lax.axis_size("x")
    pairs = []
    for d in range(nd):
        for x in range(nx):
            for c in range(2):
                along_x = (c == 0) != second
                to_d, to_x = (d, (x + step) % nx) if along_x else ((d + step) % nd, x)
                pairs.append(((d * nx + x) * 2 + c, (to_d * nx + to_x) * 2 + c))
    return lax.ppermute(a, ("dp", "x", "core"), pairs)


def dot(a, b, dims):
    return lax.dot_general(a, b, (dims, ((), ())), preferred_element_type=F32)


def add(*parts):
    out = parts[0].astype(F32)
    for p in parts[1:]:
        out = out + p.astype(F32)
    return out.astype(BF)


def tie(values, *late):
    out = lax.optimization_barrier((tuple(values), tuple(late)))
    return out[0]


def same(shape):
    return pl.BlockSpec(shape, lambda k, xi: (0,) * len(shape), pipeline_mode=pl.Buffered(1))


def call(body, grid, in_specs, out_specs, out_shape, args, flops, mib):
    return pl.pallas_call(
        body,
        grid_spec=pltpu.PrefetchScalarGridSpec(
            num_scalar_prefetch=1, grid=grid, in_specs=in_specs, out_specs=out_specs
        ),
        out_shape=out_shape,
        compiler_params=pltpu.CompilerParams(
            dimension_semantics=("arbitrary",), vmem_limit_bytes=mib << 20
        ),
        cost_estimate=pl.CostEstimate(flops=int(flops), bytes_accessed=8 << 20, transcendentals=0),
    )(*args)


def call_inside(body, out_specs, out_shape, args, flops, mib, scratch=()):
    return pl.pallas_call(
        body,
        in_specs=[SCALARS] + [INSIDE] * (len(args) - 1),
        out_specs=out_specs,
        out_shape=out_shape,
        scratch_shapes=scratch,
        compiler_params=pltpu.CompilerParams(vmem_limit_bytes=mib << 20),
        cost_estimate=pl.CostEstimate(flops=int(flops), bytes_accessed=8 << 20, transcendentals=0),
    )(*args)


def x_of(xi):
    return xi[0] // 2


def core_of(xi):
    return xi[0] % 2


def group_of(r, groups, size):
    g = jnp.zeros_like(r)
    for m in range(1, groups):
        g += (r >= m * size).astype(jnp.int32)
    return g


def dispatch(at, ids, gates, tokens, grad_out, half, slots, cols):
    experts = lax.axis_size("expert")
    every, rows = experts * slots, tokens.shape[0]

    def body(xi, ids, gates, tok, grad, sent, pick):
        j = lax.broadcasted_iota(jnp.int32, (every, 1), 0)
        e = group_of(j, experts, slots)
        j = j - e * slots
        is_x, is_y = j < half, (j >= half) & (j < 2 * half)
        s = jnp.where(is_x, j, j - half) + core_of(xi) * half
        first, second = ids[0:1, :] == e, ids[1:2, :] == e
        member = jnp.where(first | second, 1.0, 0.0)
        early = lax.broadcasted_iota(jnp.int32, (rows, rows), 0)
        late = lax.broadcasted_iota(jnp.int32, (rows, rows), 1)
        before = jnp.where(early < late, 1.0, 0.0).astype(BF)
        slot = dot(member.astype(BF), before, ((1,), (0,)))
        hit = jnp.where(slot == s.astype(F32), member, 0.0)
        hit_x, hit_y = jnp.where(is_x, hit, 0.0), jnp.where(is_y, hit, 0.0)
        gate = jnp.where(first, gates[0:1, :], 0.0) + jnp.where(second, gates[1:2, :], 0.0)
        gate = jnp.sum(hit_y * gate, axis=1, keepdims=True)
        x = dot(hit_x.astype(BF), tok[...], ((1,), (0,)))
        y = dot(hit_y.astype(BF), grad[...], ((1,), (0,))) * gate
        sent[...] = (x + y).astype(BF)
        pick[...] = (hit_x + hit_y).astype(BF)

    column = pl.BlockSpec((rows, cols), lambda k, xi: (0, x_of(xi)))
    return call(
        body,
        (1,),
        [same(ids.shape), same(gates.shape), column, column],
        [same((every, cols)), same((every, rows))],
        [jax.ShapeDtypeStruct((every, cols), BF), jax.ShapeDtypeStruct((every, rows), BF)],
        (at, ids, gates, tokens, grad_out),
        4 * every * rows * cols,
        56,
    )


def compact(at, got, experts, half):
    rows, cols = got.shape
    slots = rows // experts
    side = experts * half

    def body(xi, a, out):
        r = lax.broadcasted_iota(jnp.int32, (2 * side, 1), 0)
        is_y = (r >= side).astype(jnp.int32)
        r = r - is_y * side
        e = group_of(r, experts, half)
        place = e * slots + is_y * half + r - e * half
        q = lax.broadcasted_iota(jnp.int32, (2 * side, rows), 1)
        m = jnp.where(q == place, 1.0, 0.0).astype(BF)
        out[...] = dot(m, a[...], ((1,), (0,))).astype(BF)

    return call_inside(
        body,
        INSIDE,
        jax.ShapeDtypeStruct((2 * side, cols), BF),
        (at, got),
        4 * side * rows * cols,
        8,
    )


def spread(at, parts, experts, slots):
    side, cols = parts[0].shape
    half = side // experts
    rows = experts * slots

    def body(xi, *refs):
        *ins, out = refs
        total = ins[0][...].astype(F32)
        for a in ins[1:]:
            total += a[...].astype(F32)
        total = total.astype(BF)
        j = lax.broadcasted_iota(jnp.int32, (rows, 1), 0)
        e = group_of(j, experts, slots)
        j = j - e * slots
        q = lax.broadcasted_iota(jnp.int32, (rows, side), 1)
        low = jnp.where((q == e * half + j) & (j < half), 1.0, 0.0).astype(BF)
        high = (q == e * half + j - half) & (j >= half) & (j < 2 * half)
        high = jnp.where(high, 1.0, 0.0).astype(BF)
        out[...] = (
            dot(low, total[:, : cols // 2], ((1,), (0,)))
            + dot(high, total[:, cols // 2 :], ((1,), (0,)))
        ).astype(BF)

    return call_inside(
        body,
        INSIDE,
        jax.ShapeDtypeStruct((rows, cols // 2), BF),
        (at, *parts),
        2 * rows * side * cols,
        8,
    )


def combine(at, pick, back, experts, half):
    rows, tokens = pick.shape
    cols = back.shape[1]
    slots = rows // experts

    def body(xi, pick, back, mine, other):
        j = lax.broadcasted_iota(jnp.int32, (rows, 1), 0)
        j = j - group_of(j, experts, slots) * slots
        a = back[...]
        none = jnp.zeros_like(a)
        low = dot(pick[...], jnp.where(j < half, a, none), ((0,), (0,)))
        high = dot(pick[...], jnp.where(j >= half, a, none), ((0,), (0,)))
        on0 = core_of(xi) == 0
        mine[...] = jnp.where(on0, low, high)
        other[...] = jnp.where(on0, high, low)

    shape = jax.ShapeDtypeStruct((tokens, cols), F32)
    return call_inside(
        body, [INSIDE] * 2, [shape] * 2, (at, pick, back), 4 * rows * tokens * cols, 8
    )


def pack(at, own, theirs):
    width, hid = own[0].shape
    cols = width // 4
    up = pl.BlockSpec((cols, hid), lambda k, xi: ((x_of(xi) + k) % 4, 0))
    down = pl.BlockSpec((hid, cols), lambda k, xi: (0, (x_of(xi) + k) % 4))

    def body(xi, g1, u1, d1, g2, u2, d2, w, wd):
        for j, ref in enumerate((g1, u1, g2, u2)):
            w[0, :, j * hid : (j + 1) * hid] = ref[...]
        wd[0, :hid] = d1[...]
        wd[0, hid:] = d2[...]

    return call(
        body,
        (4,),
        [up, up, down] * 2,
        [
            pl.BlockSpec((1, cols, 4 * hid), lambda k, xi: (k, 0, 0)),
            pl.BlockSpec((1, 2 * hid, cols), lambda k, xi: (k, 0, 0)),
        ],
        [
            jax.ShapeDtypeStruct((4, cols, 4 * hid), BF),
            jax.ShapeDtypeStruct((4, 2 * hid, cols), BF),
        ],
        (at, *own, *theirs),
        width * hid,
        14,
    )


def put_in(xi, hu, ga, piece, first, s, w, wd):
    on0 = core_of(xi) == 0
    row, col = jnp.where(on0, s, first), jnp.where(on0, first, s)
    rows = hu.shape[1]
    hu[row] += dot(piece[:rows], w[col], ((1,), (0,)))
    ga[row] += dot(piece[rows:], wd[col], ((1,), (1,)))


def early_part(at, pieces, places, w, wd, so_far=None):
    n = len(pieces)
    rows = pieces[0].shape[1] // 2
    count = pieces[0].shape[0]
    more = [] if so_far is None else list(so_far)

    def body(xi, *refs):
        ps, w, wd, hu, ga = refs[:n], refs[n], refs[n + 1], refs[-2], refs[-1]
        if more:
            hu[...] = refs[n + 2][...]
            ga[...] = refs[n + 3][...]
        else:
            hu[...] = jnp.zeros_like(hu)
            ga[...] = jnp.zeros_like(ga)

        @pl.loop(0, count)
        def _(k):
            for p, (first, s) in zip(ps, places):
                put_in(xi, hu, ga, p.at[k], first + k, s, w, wd)

    shapes = [
        jax.ShapeDtypeStruct((4, rows, w.shape[2]), F32),
        jax.ShapeDtypeStruct((4, rows, wd.shape[1]), F32),
    ]
    return call_inside(
        body,
        [INSIDE] * 2,
        shapes,
        (at, *pieces, w, wd, *more),
        2 * n * count * rows * w.shape[1] * (w.shape[2] + wd.shape[1]),
        12,
    )


def token_part(at, hu, ga, p2a, p2b, w, wd):
    rows = hu.shape[1]
    cols = w.shape[1]
    hid = w.shape[2] // 4
    every = 4 * rows

    def body(xi, hu, ga, pa, pb, w, wd, act, g, keep):
        def finish(k, hu2, ga2):
            r = slice(k * rows, (k + 1) * rows)
            for c in range(2):
                part = slice(c * hid, (c + 1) * hid)
                hs = slice(2 * c * hid, (2 * c + 1) * hid)
                us = slice((2 * c + 1) * hid, (2 * c + 2) * hid)
                hh, uu, gg = hu[k, :, hs], hu[k, :, us], ga[k, :, part]
                if hu2 is not None:
                    hh, uu, gg = hh + hu2[:, hs], uu + hu2[:, us], gg + ga2[:, part]
                s = jax.nn.sigmoid(hh)
                silu = hh * s
                act[r, part] = (silu * uu).astype(BF)
                g[r, hs] = (gg * uu * (s * (1.0 + hh * (1.0 - s)))).astype(BF)
                g[r, us] = (gg * silu).astype(BF)

        last = ((pa, 0), (pa, 1), (pb, 0), (pb, 1))

        @pl.when(core_of(xi) == 0)
        def _():
            hu2 = ga2 = 0.0
            for k, (p, n) in enumerate(last):
                hu2 += dot(p[n, :rows], w[k], ((1,), (0,)))
                ga2 += dot(p[n, rows:], wd[k], ((1,), (1,)))
            for k in range(4):
                finish(k, *((hu2, ga2) if k == 2 else (None, None)))

        @pl.when(core_of(xi) == 1)
        def _():
            for k, (p, n) in enumerate(last):
                hu2 = dot(p[n, :rows], w[2], ((1,), (0,)))
                finish(k, hu2, dot(p[n, rows:], wd[2], ((1,), (1,))))

        @pl.loop(0, 4)
        def _(k):
            out = dot(g[...], w[k], ((1,), (1,))).astype(BF)

            @pl.when(core_of(xi) == 0)
            def _():
                for j in range(4):
                    keep[k, j] = out[j * rows : (j + 1) * rows]

            @pl.when(core_of(xi) == 1)
            def _():
                for j in range(4):
                    keep[j, k] = out[j * rows : (j + 1) * rows]

    return call_inside(
        body,
        [INSIDE] * 3,
        [
            jax.ShapeDtypeStruct((every, 2 * hid), BF),
            jax.ShapeDtypeStruct((every, 4 * hid), BF),
            jax.ShapeDtypeStruct((4, 4, rows, cols), BF),
        ],
        (at, hu, ga, p2a, p2b, w, wd),
        2 * every * 4 * cols * 4 * hid,
        20,
    )


def weight_part(at, pieces, act, g, which, dtype):
    p0 = pieces[0]
    rows, cols = p0.shape[1] // 2, p0.shape[2]
    every, width = 4 * rows, 4 * cols
    hid = act.shape[1] // 2
    squares = [slice(j * hid, (j + 1) * hid) for j in range(cols // hid)]

    def body(xi, p0, p1a, p1b, p2a, p2b, p3a, p3b, act, g, *refs):
        xbuf, ybuf = refs[-2:]

        def load(sources):
            for j, (ref, n) in enumerate(sources):
                xbuf[j * rows : (j + 1) * rows] = ref[n, :rows]
                ybuf[j * rows : (j + 1) * rows] = ref[n, rows:]

        def step(k):
            on0 = core_of(xi) == 0

            @pl.when(on0 & (k < 2))
            def _():
                load([(p0, k), (p1a, k), (p2a, k), (p3a, k)])

            @pl.when(on0 & (k >= 2))
            def _():
                load([(p0, k), (p1b, k - 2), (p2b, k - 2), (p3b, k - 2)])

            for n, (a, b) in enumerate(((p0, p0), (p1a, p1b), (p2a, p2b), (p3a, p3b))):

                @pl.when(jnp.logical_not(on0) & (k == n))
                def _():
                    shift = 2 if a is b else 0
                    load([(a, 0), (a, 1), (b, shift), (b, shift + 1)])

            cut = slice(which * hid, (which + 1) * hid)
            cut2 = slice(2 * which * hid, 2 * (which + 1) * hid)
            return (
                dot(xbuf[...], g[:, cut2], ((0,), (0,))),
                dot(act[:, cut], ybuf[...], ((0,), (0,))),
            )

        out = refs[0]

        @pl.loop(0, 4)
        def _(k):
            up, down = step(k)
            out[k, :, : 2 * hid] = up.astype(out.dtype)
            for c in squares:
                out[k, c, 2 * hid :] = down[:, c].astype(out.dtype)

    return call_inside(
        body,
        INSIDE,
        jax.ShapeDtypeStruct((4, cols, 3 * hid), dtype),
        (at, *pieces, act, g),
        2 * 3 * every * width * hid,
        14,
        [pltpu.VMEM((every, cols), BF)] * 2,
    )


def weight_sum(at, mine, other):
    _, cols, hid = mine.shape
    hid //= 3
    width = 4 * cols

    def body(xi, mine, other, og, ou, od, sg, su, sd, sems):
        def copies(k):
            block = pl.ds(pl.multiple_of((x_of(xi) + k) % 4 * cols, cols), cols)
            return (
                pltpu.make_async_copy(sg.at[k], og.at[block, :], sems.at[k, 0]),
                pltpu.make_async_copy(su.at[k], ou.at[block, :], sems.at[k, 1]),
                pltpu.make_async_copy(sd.at[k], od.at[:, block], sems.at[k, 2]),
            )

        @pl.loop(0, 4)
        def _(k):
            total = (mine[k] + other[k].astype(F32)).astype(BF)
            sg[k] = total[:, :hid]
            su[k] = total[:, hid : 2 * hid]
            for j in range(cols // hid):
                c = slice(j * hid, (j + 1) * hid)
                sd[k, :, c] = total[c, 2 * hid :]
            for copy in copies(k):
                copy.start()

        @pl.loop(0, 4)
        def _(k):
            for copy in copies(k):
                copy.wait()

    return call_inside(
        body,
        [pl.BlockSpec(memory_space=pl.ANY)] * 3,
        [
            jax.ShapeDtypeStruct((width, hid), BF),
            jax.ShapeDtypeStruct((width, hid), BF),
            jax.ShapeDtypeStruct((hid, width), BF),
        ],
        (at, mine, other),
        12 * width * hid,
        14,
        [
            pltpu.VMEM((4, cols, hid), BF),
            pltpu.VMEM((4, cols, hid), BF),
            pltpu.VMEM((4, hid, cols), BF),
            pltpu.SemaphoreType.DMA((4, 3)),
        ],
    )


def shards(tokens, grad_out, gate_prob, expert_ids, w_gate, w_up, w_down):
    rows, width = tokens.shape
    experts = lax.axis_size("expert")
    capacity = rows * 9 // (4 * experts)
    half = capacity // 2
    cols = width // lax.axis_size("x")
    slots = (capacity + 7) // 8 * 8
    at = lax.axis_index(("x", "core")).astype(jnp.int32).reshape(1)
    own = (w_gate[0], w_up[0], w_down[0])
    theirs = [swap(w) for w in own]

    def exchange(a):
        a = a.reshape(experts, slots, -1)
        a = lax.all_to_all(a, "expert", split_axis=0, concat_axis=0, tiled=True)
        return a.reshape(experts * slots, -1)

    sent, pick = dispatch(at, expert_ids.T, gate_prob.T, tokens, grad_out, half, slots, cols)
    (got,) = tie((exchange(sent),), *theirs)
    got = compact(at, got, experts, half)
    w, wd = pack(at, own, theirs)

    p0 = jnp.stack([got, ring(got, False, -1), ring(got, False, 2), ring(got, False, 1)])
    p1a, p3b = ring(p0[:2], True, -1), ring(p0[2:], True, 1)
    p1b, p3a = ring(p0[2:], True, -1), ring(p0[:2], True, 1)
    early = early_part(at, (p0,), ((0, 0),), w, wd)
    p1a, p3b = tie((p1a, p3b), *early)
    p2a, p2b = ring(p1a, True, -1), ring(p3b, True, 1)
    places = ((0, 1), (2, 1), (0, 3), (2, 3))
    hu, ga = early_part(at, (p1a, p1b, p3a, p3b), places, w, wd, early)
    p2a, p2b = tie((p2a, p2b), hu, ga)
    act, g, keep = token_part(at, hu, ga, p2a, p2b, w, wd)
    pieces = (p0, p1a, p1b, p2a, p2b, p3a, p3b)

    k_up, v_dn = ring(keep[2, :2], False, 1), ring(keep[2, 2:], False, -1)
    part = weight_part(at, pieces, act, g, 1, BF)
    k_up, v_dn, part, keep = tie((k_up, v_dn, part, keep))
    k_up, v_dn = tie((add(keep[1, :2], k_up), add(keep[3, 2:], v_dn)))
    k_up, v_dn = ring(k_up, False, 1), ring(v_dn, False, -1)
    v_up, k_dn = ring(keep[1, 2:], False, 1), ring(keep[3, :2], False, -1)
    part = swap(part)
    mine = weight_part(at, pieces, act, g, 0, F32)
    k_up, v_dn, v_up, k_dn = tie((k_up, v_dn, v_up, k_dn), mine)
    total = jnp.concatenate([add(keep[0, :2], k_up, k_dn), add(keep[0, 2:], v_up, v_dn)], axis=0)
    parts = [ring(total[k], True, k) for k in (1, 2, 3)]
    gw_gate, gw_up, gw_down = weight_sum(at, mine, part)
    parts = tie(parts, gw_gate)

    back = exchange(spread(at, [total[0], *parts], experts, slots))
    mine, other = combine(at, pick, back, experts, half)
    grad_tokens = (mine + swap(other)).astype(BF)
    return grad_tokens, gw_gate[None], gw_up[None], gw_down[None]


def solution(mesh):
    sizes = mesh.devices.shape
    fine = Mesh(
        mesh.devices.reshape(sizes[0], sizes[1], sizes[2] // 2, 2), ("dp", "expert", "x", "core")
    )
    by_token = P(("dp", "expert"), None)
    up = P("expert", None, ("dp", "x", "core"))
    down = P("expert", ("dp", "x", "core"), None)
    return jax.shard_map(
        shards,
        mesh=fine,
        in_specs=(by_token, by_token, by_token, by_token, up, up, down),
        out_specs=(P(("dp", "expert"), ("x", "core")), up, up, down),
        check_vma=False,
    )
```

profile of v0, /device:TPU:1, one launch (start us, length us, event | category | flops | bytes accessed | tf_op | source)
XLA Modules:
  0.0 139.7 jit_solution(15810841386918964689)
XLA Ops:
  0.6 3.3 %collective-permute-start = (bf16[3072,256]{1,0:T(8,128)(2,1)}, bf16[3072,256]{1,0:T(8,128)(2,1)S(1)}, u32[]{:S(2)}, u32[]{:S(2)}) collective-permute-start(bf16[3072,256]{1,0:T(8,128)(2,1)} %bitcast.48), channel_id=1, source_target_pairs={{0,1},{1,0},{2,3},{3,2},{4,5},{5,4},{6,7},{7,6},{8,9},{9,8},{10,11... | collective-permute-start | bytes 4718600 | tf_op jit(solution)/shard_map/ppermute | solution.py:15
  4.1 0.4 collective-permute-start.2
  4.5 2.4 %shard_map.102 = (bf16[320,768]{1,0:T(8,128)(2,1)}, bf16[320,128]{1,0:T(8,128)(2,1)}) custom-call(s32[1]{0:T(128)} %bitcast.xi, s32[2,128]{1,0:T(2,128)} %bitcast.63, f32[2,128]{1,0:T(2,128)} %bitcast.64, bf16[128,3072]{1,0:T(8,128)(2,1)} %tok.1, bf16[128,3072]{1,0:T(8,128)(2,1)} %grad.1), custom_call_target="tpu_custom_call" | custom-call | flops 125829120 | bytes 8388608 | tf_op jit(solution)/shard_map/pallas_call | solution.py:51
  6.8 23.9 %all_to_all.10 = bf16[8,40,768]{2,1,0:T(8,128)(2,1)S(1)} all-to-all(bf16[8,40,768]{2,1,0:T(8,128)(2,1)} %bitcast.62), channel_id=1, replica_groups=mesh['dp'=4,'expert'=8,'x'=4,'core'=2] {'expert'}, dimensions={0} | all-to-all | bytes 983040 | tf_op jit(solution)/shard_map/all_to_all | solution.py:471
  30.7 0.4 shard_map.103
  31.1 3.0 %collective-permute-start.5 = (bf16[288,768]{1,0:T(8,128)(2,1)S(1)}, bf16[288,768]{1,0:T(8,128)(2,1)S(1)}, u32[]{:S(2)}, u32[]{:S(2)}) collective-permute-start(bf16[288,768]{1,0:T(8,128)(2,1)S(1)} %shard_map.103), channel_id=1, source_target_pairs={{0,4},{1,129},{2,6},{3,131},{4,0},{5,133},{6,2},{7,135},{64,68},{6... | collective-permute-start | bytes 1327112 | tf_op jit(solution)/shard_map/ppermute | solution.py:27
  34.1 0.4 collective-permute-start.6
  34.5 2.3 %collective-permute-start.3 = (bf16[288,768]{1,0:T(8,128)(2,1)S(1)}, bf16[288,768]{1,0:T(8,128)(2,1)S(1)}, u32[]{:S(2)}, u32[]{:S(2)}) collective-permute-start(bf16[288,768]{1,0:T(8,128)(2,1)S(1)} %shard_map.103), channel_id=1, source_target_pairs={{0,6},{1,193},{2,0},{3,195},{4,2},{5,197},{6,4},{7,199},{64,70},{6... | collective-permute-start | bytes 1327112 | tf_op jit(solution)/shard_map/ppermute | solution.py:27
  36.8 3.4 %collective-permute-done.5 = bf16[288,768]{1,0:T(8,128)(2,1)S(1)} collective-permute-done((bf16[288,768]{1,0:T(8,128)(2,1)S(1)}, bf16[288,768]{1,0:T(8,128)(2,1)S(1)}, u32[]{:S(2)}, u32[]{:S(2)}) %collective-permute-start.5) | collective-permute-done | bytes 442400 | tf_op jit(solution)/shard_map/ppermute | solution.py:27
  40.2 4.7 %collective-permute-done.6 = bf16[288,768]{1,0:T(8,128)(2,1)S(1)} collective-permute-done((bf16[288,768]{1,0:T(8,128)(2,1)S(1)}, bf16[288,768]{1,0:T(8,128)(2,1)S(1)}, u32[]{:S(2)}, u32[]{:S(2)}) %collective-permute-start.6) | collective-permute-done | bytes 442400 | tf_op jit(solution)/shard_map/ppermute | solution.py:27
  45.0 1.0 collective-permute-start.7
  46.1 1.8 %collective-permute-start.4 = (bf16[2,288,768]{2,1,0:T(8,128)(2,1)S(1)}, bf16[2,288,768]{2,1,0:T(8,128)(2,1)S(1)}, u32[]{:S(2)}, u32[]{:S(2)}) collective-permute-start(bf16[2,288,768]{2,1,0:T(8,128)(2,1)S(1)} %pad_maximum_fusion.1), channel_id=1, source_target_pairs={{0,192},{1,7},{2,194},{3,1},{4,196},{5,3},{6,198},{7,5},{64,0},{65... | collective-permute-start | bytes 2654216 | tf_op jit(solution)/shard_map/ppermute | solution.py:27
  47.9 3.1 %shard_map.104 = (bf16[4,768,1024]{2,1,0:T(8,128)(2,1)S(1)}, bf16[4,512,768]{2,1,0:T(8,128)(2,1)S(1)}) custom-call(s32[1]{0:T(128)} %bitcast.xi, bf16[3072,256]{1,0:T(8,128)(2,1)S(1)} %bitcast.49, bf16[3072,256]{1,0:T(8,128)(2,1)S(1)} %bitcast.51, bf16[256,3072]{1,0:T(8,128)(2,1)S(1)} %bitcast.53, bf16[3072,256]{1,0:T(8,128)(2,1)S(1)} %collective-permute-done.g2, ...), custom_call_target="tpu_custom_call" | custom-call | flops 786432 | bytes 8388608 | tf_op jit(solution)/shard_map/pallas_call | solution.py:51
  51.1 1.4 collective-permute-start.8
  52.4 0.2 collective-permute-start.9
  52.6 0.2 pad_maximum_fusion.refs_0_.p0
  52.8 2.9 %shard_map.105 = (f32[4,144,1024]{2,1,0:T(8,128)S(1)}, f32[4,144,512]{2,1,0:T(8,128)S(1)}) custom-call(s32[1]{0:T(128)} %bitcast.xi, bf16[4,288,768]{2,1,0:T(8,128)(2,1)S(1)} %pad_maximum_fusion.refs_0_.p0, bf16[4,768,1024]{2,1,0:T(8,128)(2,1)S(1)} %get-tuple-element.41.refs_1_.refs_4_.w, bf16[4,512,768]{2,1,0:T(8,128)(2,1)S(1)} %get-tuple-element.42.refs_2_.refs_5_.wd), custom_call_target="tpu_custom_call" | custom-call | flops 1358954496 | bytes 8388608 | tf_op jit(solution)/shard_map/pallas_call | solution.py:65
  55.7 2.8 %collective-permute-done.7.refs_3_.p3b = bf16[2,288,768]{2,1,0:T(8,128)(2,1)S(1)} collective-permute-done((bf16[2,288,768]{2,1,0:T(8,128)(2,1)S(1)}, bf16[2,288,768]{2,1,0:T(8,128)(2,1)S(1)}, u32[]{:S(2)}, u32[]{:S(2)}) %collective-permute-start.7) | collective-permute-done | bytes 884768 | tf_op jit(solution)/shard_map/ppermute | solution.py:27
  58.5 2.8 %collective-permute-start.10 = (bf16[2,288,768]{2,1,0:T(8,128)(2,1)S(1)}, bf16[2,288,768]{2,1,0:T(8,128)(2,1)S(1)}, u32[]{:S(2)}, u32[]{:S(2)}) collective-permute-start(bf16[2,288,768]{2,1,0:T(8,128)(2,1)S(1)} %collective-permute-done.4.refs_0_.p1a), channel_id=1, source_target_pairs={{0,192},{1,7},{2,194},{3,1},{4,196},{5,3},{6,198},{7,5},{64,0},{65... | collective-permute-start | bytes 2654216 | tf_op jit(solution)/shard_map/ppermute | solution.py:27
  61.3 6.5 %collective-permute-done.8.refs_1_.p1b = bf16[2,288,768]{2,1,0:T(8,128)(2,1)S(1)} collective-permute-done((bf16[2,288,768]{2,1,0:T(8,128)(2,1)S(1)}, bf16[2,288,768]{2,1,0:T(8,128)(2,1)S(1)}, u32[]{:S(2)}, u32[]{:S(2)}) %collective-permute-start.8) | collective-permute-done | bytes 884768 | tf_op jit(solution)/shard_map/ppermute | solution.py:27
  67.9 4.5 %shard_map.106 = (f32[4,144,1024]{2,1,0:T(8,128)S(1)}, f32[4,144,512]{2,1,0:T(8,128)S(1)}) custom-call(s32[1]{0:T(128)} %bitcast.xi, bf16[2,288,768]{2,1,0:T(8,128)(2,1)S(1)} %collective-permute-done.4.refs_0_.p1a, bf16[2,288,768]{2,1,0:T(8,128)(2,1)S(1)} %collective-permute-done.8.refs_1_.p1b, bf16[2,288,768]{2,1,0:T(8,128)(2,1)S(1)} %collective-permute-done.9.refs_2_.p3a, ...), custom_call_target="tpu_custom_call" | custom-call | flops 2717908992 | bytes 8388608 | tf_op jit(solution)/shard_map/pallas_call | solution.py:65
  72.5 4.8 %collective-permute-done.10.pa.p2a = bf16[2,288,768]{2,1,0:T(8,128)(2,1)S(1)} collective-permute-done((bf16[2,288,768]{2,1,0:T(8,128)(2,1)S(1)}, bf16[2,288,768]{2,1,0:T(8,128)(2,1)S(1)}, u32[]{:S(2)}, u32[]{:S(2)}) %collective-permute-start.10) | collective-permute-done | bytes 884768 | tf_op jit(solution)/shard_map/ppermute | solution.py:27
  77.4 7.2 %shard_map.107 = (bf16[576,512]{1,0:T(8,128)(2,1)S(1)}, bf16[576,1024]{1,0:T(8,128)(2,1)S(1)}, bf16[4,4,144,768]{3,2,1,0:T(8,128)(2,1)S(1)}) custom-call(s32[1]{0:T(128)} %bitcast.xi, f32[4,144,1024]{2,1,0:T(8,128)S(1)} %get-tuple-element.47.hu, f32[4,144,512]{2,1,0:T(8,128)S(1)} %get-tuple-element.48.ga, ...), custom_call_target="tpu_custom_call" | custom-call | flops 3623878656 | bytes 8388608 | tf_op jit(solution)/shard_map/pallas_call | solution.py:65
  84.7 1.7 %collective-permute-start.12 = (bf16[2,144,768]{2,1,0:T(8,128)(2,1)S(1)}, bf16[2,144,768]{2,1,0:T(8,128)(2,1)S(1)}, u32[]{:S(2)}, u32[]{:S(2)}) collective-permute-start(bf16[2,144,768]{2,1,0:T(8,128)(2,1)S(1)} %get-tuple-element.79), channel_id=1, source_target_pairs={{0,2},{1,65},{2,4},{3,67},{4,6},{5,69},{6,0},{7,71},{64,66},{65,12... | collective-permute-start | bytes 1327112 | tf_op jit(solution)/shard_map/ppermute | solution.py:27
  86.4 1.1 collective-permute-start.13
  87.5 5.1 %shard_map.108 = bf16[4,768,768]{2,1,0:T(8,128)(2,1)S(1)} custom-call(s32[1]{0:T(128)} %bitcast.xi, bf16[4,288,768]{2,1,0:T(8,128)(2,1)S(1)} %pad_maximum_fusion.refs_0_.p0, bf16[2,288,768]{2,1,0:T(8,128)(2,1)S(1)} %collective-permute-done.4.refs_0_.p1a, bf16[2,288,768]{2,1,0:T(8,128)(2,1)S(1)} %collective-permute-done.8.refs_1_.p1b, ...), custom_call_target="tpu_custom_call" | custom-call | flops 2717908992 | bytes 8388608 | tf_op jit(solution)/shard_map/pallas_call | solution.py:65
  92.6 0.8 collective-permute-done.12
  93.5 0.4 collective-permute-done.13
  93.9 4.0 %collective-permute-start.21 = (bf16[4,768,768]{2,1,0:T(8,128)(2,1)S(1)}, bf16[4,768,768]{2,1,0:T(8,128)(2,1)S(1)}, u32[]{:S(2)}, u32[]{:S(2)}) collective-permute-start(bf16[4,768,768]{2,1,0:T(8,128)(2,1)S(1)} %shard_map.108), channel_id=1, source_target_pairs={{0,1},{1,0},{2,3},{3,2},{4,5},{5,4},{6,7},{7,6},{8,9},{9,8},{10,11... | collective-permute-start | bytes 14155784 | tf_op jit(solution)/shard_map/ppermute | solution.py:15
  97.8 0.2 fusion.2
  98.1 1.4 collective-permute-start.14
  99.4 1.7 %collective-permute-start.15 = (bf16[2,144,768]{2,1,0:T(8,128)(2,1)S(1)}, bf16[2,144,768]{2,1,0:T(8,128)(2,1)S(1)}, u32[]{:S(2)}, u32[]{:S(2)}) collective-permute-start(bf16[2,144,768]{2,1,0:T(8,128)(2,1)S(1)} %get-tuple-element.58), channel_id=1, source_target_pairs={{0,6},{1,193},{2,0},{3,195},{4,2},{5,197},{6,4},{7,199},{64,70},{6... | collective-permute-start | bytes 1327112 | tf_op jit(solution)/shard_map/ppermute | solution.py:27
  101.2 0.3 collective-permute-start.16
  101.5 2.7 %collective-permute-start.17 = (bf16[2,144,768]{2,1,0:T(8,128)(2,1)S(1)}, bf16[2,144,768]{2,1,0:T(8,128)(2,1)S(1)}, u32[]{:S(2)}, u32[]{:S(2)}) collective-permute-start(bf16[2,144,768]{2,1,0:T(8,128)(2,1)S(1)} %get-tuple-element.74), channel_id=1, source_target_pairs={{0,6},{1,193},{2,0},{3,195},{4,2},{5,197},{6,4},{7,199},{64,70},{6... | collective-permute-start | bytes 1327112 | tf_op jit(solution)/shard_map/ppermute | solution.py:27
  104.1 5.2 %shard_map.109.mine = f32[4,768,768]{2,1,0:T(8,128)S(1)} custom-call(s32[1]{0:T(128)} %bitcast.xi, bf16[4,288,768]{2,1,0:T(8,128)(2,1)S(1)} %pad_maximum_fusion.refs_0_.p0, bf16[2,288,768]{2,1,0:T(8,128)(2,1)S(1)} %collective-permute-done.4.refs_0_.p1a, bf16[2,288,768]{2,1,0:T(8,128)(2,1)S(1)} %collective-permute-done.8.refs_1_.p1b, ...), custom_call_target="tpu_custom_call" | custom-call | flops 2717908992 | bytes 8388608 | tf_op jit(solution)/shard_map/pallas_call | solution.py:65
  109.3 2.4 %collective-permute-done.16 = bf16[2,144,768]{2,1,0:T(8,128)(2,1)S(1)} collective-permute-done((bf16[2,144,768]{2,1,0:T(8,128)(2,1)S(1)}, bf16[2,144,768]{2,1,0:T(8,128)(2,1)S(1)}, u32[]{:S(2)}, u32[]{:S(2)}) %collective-permute-start.16) | collective-permute-done | bytes 442400 | tf_op jit(solution)/shard_map/ppermute | solution.py:27
  111.7 0.3 fusion.1
  112.1 0.2 collective-permute-start.18
  112.4 3.6 %collective-permute-start.19 = (bf16[144,768]{1,0:T(8,128)(2,1)S(1)}, bf16[144,768]{1,0:T(8,128)(2,1)S(1)}, u32[]{:S(2)}, u32[]{:S(2)}) collective-permute-start(bf16[144,768]{1,0:T(8,128)(2,1)S(1)} %get-tuple-element.81), channel_id=1, source_target_pairs={{0,128},{1,5},{2,130},{3,7},{4,132},{5,1},{6,134},{7,3},{64,192},{... | collective-permute-start | bytes 663560 | tf_op jit(solution)/shard_map/ppermute | solution.py:27
  116.0 2.3 %shard_map.110 = (bf16[3072,256]{1,0:T(8,128)(2,1)}, bf16[3072,256]{1,0:T(8,128)(2,1)}, bf16[256,3072]{1,0:T(8,128)(2,1)}) custom-call(s32[1]{0:T(128)} %bitcast.xi, f32[4,768,768]{2,1,0:T(8,128)S(1)} %shard_map.109.mine, bf16[4,768,768]{2,1,0:T(8,128)(2,1)S(1)} %collective-permute-done.21.other), custom_call_target="tpu_custom_call" | custom-call | flops 9437184 | bytes 8388608 | tf_op jit(solution)/shard_map/pallas_call | solution.py:65
  118.3 0.1 collective-permute-done.18.refs_1_
  118.5 3.4 %collective-permute-done.19.refs_2_ = bf16[144,768]{1,0:T(8,128)(2,1)S(1)} collective-permute-done((bf16[144,768]{1,0:T(8,128)(2,1)S(1)}, bf16[144,768]{1,0:T(8,128)(2,1)S(1)}, u32[]{:S(2)}, u32[]{:S(2)}) %collective-permute-start.19) | collective-permute-done | bytes 221216 | tf_op jit(solution)/shard_map/ppermute | solution.py:27
  121.8 0.4 shard_map.111
  122.2 11.8 %all_to_all.11 = bf16[8,40,384]{2,1,0:T(8,128)(2,1)S(1)} all-to-all(bf16[8,40,384]{2,1,0:T(8,128)(2,1)S(1)} %bitcast.55), channel_id=1, replica_groups=mesh['dp'=4,'expert'=8,'x'=4,'core'=2] {'expert'}, dimensions={0} | all-to-all | bytes 491520 | tf_op jit(solution)/shard_map/all_to_all | solution.py:471
  134.0 0.3 shard_map.112
  134.4 3.6 %collective-permute-start.22 = (f32[128,384]{1,0:T(8,128)S(1)}, f32[128,384]{1,0:T(8,128)S(1)}, u32[]{:S(2)}, u32[]{:S(2)}) collective-permute-start(f32[128,384]{1,0:T(8,128)S(1)} %get-tuple-element.69), channel_id=1, source_target_pairs={{0,1},{1,0},{2,3},{3,2},{4,5},{5,4},{6,7},{7,6},{8,9},{9,8},{10,11... | collective-permute-start | bytes 589832 | tf_op jit(solution)/shard_map/ppermute | solution.py:15
  138.0 1.1 collective-permute-done.22
  139.0 0.7 add_convert_fusion
  (29 shorter events, 0.7 us)
Async XLA Ops:
  0.6 30.1 %collective-permute-start = (bf16[3072,256]{1,0:T(8,128)(2,1)}, bf16[3072,256]{1,0:T(8,128)(2,1)S(1)}, u32[]{:S(2)}, u32[]{:S(2)}) collective-permute-start(bf16[3072,256]{1,0:T(8,128)(2,1)} %bitcast.48), channel_id=1, source_target_pairs={{0,1},{1,0},{2,3},{3,2},{4,5},{5,4},{6,7},{7,6},{8,9},{9,8},{10,11... | collective-permute-start | bytes 4718600 | tf_op jit(solution)/shard_map/ppermute | solution.py:15
  4.0 26.8 %collective-permute-start.1 = (bf16[3072,256]{1,0:T(8,128)(2,1)}, bf16[3072,256]{1,0:T(8,128)(2,1)S(1)}, u32[]{:S(2)}, u32[]{:S(2)}) collective-permute-start(bf16[3072,256]{1,0:T(8,128)(2,1)} %bitcast.50), channel_id=1, source_target_pairs={{0,1},{1,0},{2,3},{3,2},{4,5},{5,4},{6,7},{7,6},{8,9},{9,8},{10,11... | collective-permute-start | bytes 4718600 | tf_op jit(solution)/shard_map/ppermute | solution.py:15
  4.1 26.7 %collective-permute-start.2 = (bf16[256,3072]{1,0:T(8,128)(2,1)}, bf16[256,3072]{1,0:T(8,128)(2,1)}, u32[]{:S(2)}, u32[]{:S(2)}) collective-permute-start(bf16[256,3072]{1,0:T(8,128)(2,1)} %bitcast.52), channel_id=1, source_target_pairs={{0,1},{1,0},{2,3},{3,2},{4,5},{5,4},{6,7},{7,6},{8,9},{9,8},{10,11... | collective-permute-start | bytes 4718600 | tf_op jit(solution)/shard_map/ppermute | solution.py:15
  6.8 41.1 %copy-start.2 = (bf16[1,256,3072]{2,1,0:T(8,128)(2,1)S(1)}, bf16[1,256,3072]{2,1,0:T(8,128)(2,1)}, u32[]{:S(2)}) copy-start(bf16[1,256,3072]{2,1,0:T(8,128)(2,1)} %param.13) | copy-start | bytes 4718596
  31.1 9.1 %collective-permute-start.5 = (bf16[288,768]{1,0:T(8,128)(2,1)S(1)}, bf16[288,768]{1,0:T(8,128)(2,1)S(1)}, u32[]{:S(2)}, u32[]{:S(2)}) collective-permute-start(bf16[288,768]{1,0:T(8,128)(2,1)S(1)} %shard_map.103), channel_id=1, source_target_pairs={{0,4},{1,129},{2,6},{3,131},{4,0},{5,133},{6,2},{7,135},{64,68},{6... | collective-permute-start | bytes 1327112 | tf_op jit(solution)/shard_map/ppermute | solution.py:27
  34.1 10.8 %collective-permute-start.6 = (bf16[288,768]{1,0:T(8,128)(2,1)S(1)}, bf16[288,768]{1,0:T(8,128)(2,1)S(1)}, u32[]{:S(2)}, u32[]{:S(2)}) collective-permute-start(bf16[288,768]{1,0:T(8,128)(2,1)S(1)} %shard_map.103), channel_id=1, source_target_pairs={{0,2},{1,65},{2,4},{3,67},{4,6},{5,69},{6,0},{7,71},{64,66},{65,12... | collective-permute-start | bytes 1327112 | tf_op jit(solution)/shard_map/ppermute | solution.py:27
  34.5 11.5 %collective-permute-start.3 = (bf16[288,768]{1,0:T(8,128)(2,1)S(1)}, bf16[288,768]{1,0:T(8,128)(2,1)S(1)}, u32[]{:S(2)}, u32[]{:S(2)}) collective-permute-start(bf16[288,768]{1,0:T(8,128)(2,1)S(1)} %shard_map.103), channel_id=1, source_target_pairs={{0,6},{1,193},{2,0},{3,195},{4,2},{5,197},{6,4},{7,199},{64,70},{6... | collective-permute-start | bytes 1327112 | tf_op jit(solution)/shard_map/ppermute | solution.py:27
  44.9 3.0 %copy-start = (bf16[1,3072,256]{2,1,0:T(8,128)(2,1)S(1)}, bf16[1,3072,256]{2,1,0:T(8,128)(2,1)}, u32[]{:S(2)}) copy-start(bf16[1,3072,256]{2,1,0:T(8,128)(2,1)} %param.11) | copy-start | bytes 4718596
  44.9 3.0 %copy-start.1 = (bf16[1,3072,256]{2,1,0:T(8,128)(2,1)S(1)}, bf16[1,3072,256]{2,1,0:T(8,128)(2,1)}, u32[]{:S(2)}) copy-start(bf16[1,3072,256]{2,1,0:T(8,128)(2,1)} %param.12) | copy-start | bytes 4718596
  45.0 13.5 %collective-permute-start.7 = (bf16[2,288,768]{2,1,0:T(8,128)(2,1)S(1)}, bf16[2,288,768]{2,1,0:T(8,128)(2,1)S(1)}, u32[]{:S(2)}, u32[]{:S(2)}) collective-permute-start(bf16[2,288,768]{2,1,0:T(8,128)(2,1)S(1)} %pad_maximum_fusion.2), channel_id=1, source_target_pairs={{0,64},{1,3},{2,66},{3,5},{4,68},{5,7},{6,70},{7,1},{64,128},{65,6... | collective-permute-start | bytes 2654216 | tf_op jit(solution)/shard_map/ppermute | solution.py:27
  46.1 12.4 %collective-permute-start.4 = (bf16[2,288,768]{2,1,0:T(8,128)(2,1)S(1)}, bf16[2,288,768]{2,1,0:T(8,128)(2,1)S(1)}, u32[]{:S(2)}, u32[]{:S(2)}) collective-permute-start(bf16[2,288,768]{2,1,0:T(8,128)(2,1)S(1)} %pad_maximum_fusion.1), channel_id=1, source_target_pairs={{0,192},{1,7},{2,194},{3,1},{4,196},{5,3},{6,198},{7,5},{64,0},{65... | collective-permute-start | bytes 2654216 | tf_op jit(solution)/shard_map/ppermute | solution.py:27
  51.1 16.8 %collective-permute-start.8 = (bf16[2,288,768]{2,1,0:T(8,128)(2,1)S(1)}, bf16[2,288,768]{2,1,0:T(8,128)(2,1)S(1)}, u32[]{:S(2)}, u32[]{:S(2)}) collective-permute-start(bf16[2,288,768]{2,1,0:T(8,128)(2,1)S(1)} %pad_maximum_fusion.2), channel_id=1, source_target_pairs={{0,192},{1,7},{2,194},{3,1},{4,196},{5,3},{6,198},{7,5},{64,0},{65... | collective-permute-start | bytes 2654216 | tf_op jit(solution)/shard_map/ppermute | solution.py:27
  52.4 15.5 %collective-permute-start.9 = (bf16[2,288,768]{2,1,0:T(8,128)(2,1)S(1)}, bf16[2,288,768]{2,1,0:T(8,128)(2,1)S(1)}, u32[]{:S(2)}, u32[]{:S(2)}) collective-permute-start(bf16[2,288,768]{2,1,0:T(8,128)(2,1)S(1)} %pad_maximum_fusion.1), channel_id=1, source_target_pairs={{0,64},{1,3},{2,66},{3,5},{4,68},{5,7},{6,70},{7,1},{64,128},{65,6... | collective-permute-start | bytes 2654216 | tf_op jit(solution)/shard_map/ppermute | solution.py:27
  58.5 18.8 %collective-permute-start.10 = (bf16[2,288,768]{2,1,0:T(8,128)(2,1)S(1)}, bf16[2,288,768]{2,1,0:T(8,128)(2,1)S(1)}, u32[]{:S(2)}, u32[]{:S(2)}) collective-permute-start(bf16[2,288,768]{2,1,0:T(8,128)(2,1)S(1)} %collective-permute-done.4.refs_0_.p1a), channel_id=1, source_target_pairs={{0,192},{1,7},{2,194},{3,1},{4,196},{5,3},{6,198},{7,5},{64,0},{65... | collective-permute-start | bytes 2654216 | tf_op jit(solution)/shard_map/ppermute | solution.py:27
  61.3 16.1 %collective-permute-start.11 = (bf16[2,288,768]{2,1,0:T(8,128)(2,1)S(1)}, bf16[2,288,768]{2,1,0:T(8,128)(2,1)S(1)}, u32[]{:S(2)}, u32[]{:S(2)}) collective-permute-start(bf16[2,288,768]{2,1,0:T(8,128)(2,1)S(1)} %collective-permute-done.7.refs_3_.p3b), channel_id=1, source_target_pairs={{0,64},{1,3},{2,66},{3,5},{4,68},{5,7},{6,70},{7,1},{64,128},{65,6... | collective-permute-start | bytes 2654216 | tf_op jit(solution)/shard_map/ppermute | solution.py:27
  84.7 8.7 %collective-permute-start.12 = (bf16[2,144,768]{2,1,0:T(8,128)(2,1)S(1)}, bf16[2,144,768]{2,1,0:T(8,128)(2,1)S(1)}, u32[]{:S(2)}, u32[]{:S(2)}) collective-permute-start(bf16[2,144,768]{2,1,0:T(8,128)(2,1)S(1)} %get-tuple-element.79), channel_id=1, source_target_pairs={{0,2},{1,65},{2,4},{3,67},{4,6},{5,69},{6,0},{7,71},{64,66},{65,12... | collective-permute-start | bytes 1327112 | tf_op jit(solution)/shard_map/ppermute | solution.py:27
  86.4 7.4 %collective-permute-start.13 = (bf16[2,144,768]{2,1,0:T(8,128)(2,1)S(1)}, bf16[2,144,768]{2,1,0:T(8,128)(2,1)S(1)}, u32[]{:S(2)}, u32[]{:S(2)}) collective-permute-start(bf16[2,144,768]{2,1,0:T(8,128)(2,1)S(1)} %get-tuple-element.78), channel_id=1, source_target_pairs={{0,6},{1,193},{2,0},{3,195},{4,2},{5,197},{6,4},{7,199},{64,70},{6... | collective-permute-start | bytes 1327112 | tf_op jit(solution)/shard_map/ppermute | solution.py:27
  93.9 22.1 %collective-permute-start.21 = (bf16[4,768,768]{2,1,0:T(8,128)(2,1)S(1)}, bf16[4,768,768]{2,1,0:T(8,128)(2,1)S(1)}, u32[]{:S(2)}, u32[]{:S(2)}) collective-permute-start(bf16[4,768,768]{2,1,0:T(8,128)(2,1)S(1)} %shard_map.108), channel_id=1, source_target_pairs={{0,1},{1,0},{2,3},{3,2},{4,5},{5,4},{6,7},{7,6},{8,9},{9,8},{10,11... | collective-permute-start | bytes 14155784 | tf_op jit(solution)/shard_map/ppermute | solution.py:15
  98.1 11.2 %collective-permute-start.14 = (bf16[2,144,768]{2,1,0:T(8,128)(2,1)S(1)}, bf16[2,144,768]{2,1,0:T(8,128)(2,1)S(1)}, u32[]{:S(2)}, u32[]{:S(2)}) collective-permute-start(bf16[2,144,768]{2,1,0:T(8,128)(2,1)S(1)} %get-tuple-element.57), channel_id=1, source_target_pairs={{0,2},{1,65},{2,4},{3,67},{4,6},{5,69},{6,0},{7,71},{64,66},{65,12... | collective-permute-start | bytes 1327112 | tf_op jit(solution)/shard_map/ppermute | solution.py:27
  99.4 9.9 %collective-permute-start.15 = (bf16[2,144,768]{2,1,0:T(8,128)(2,1)S(1)}, bf16[2,144,768]{2,1,0:T(8,128)(2,1)S(1)}, u32[]{:S(2)}, u32[]{:S(2)}) collective-permute-start(bf16[2,144,768]{2,1,0:T(8,128)(2,1)S(1)} %get-tuple-element.58), channel_id=1, source_target_pairs={{0,6},{1,193},{2,0},{3,195},{4,2},{5,197},{6,4},{7,199},{64,70},{6... | collective-permute-start | bytes 1327112 | tf_op jit(solution)/shard_map/ppermute | solution.py:27
  101.2 10.6 %collective-permute-start.16 = (bf16[2,144,768]{2,1,0:T(8,128)(2,1)S(1)}, bf16[2,144,768]{2,1,0:T(8,128)(2,1)S(1)}, u32[]{:S(2)}, u32[]{:S(2)}) collective-permute-start(bf16[2,144,768]{2,1,0:T(8,128)(2,1)S(1)} %get-tuple-element.75), channel_id=1, source_target_pairs={{0,2},{1,65},{2,4},{3,67},{4,6},{5,69},{6,0},{7,71},{64,66},{65,12... | collective-permute-start | bytes 1327112 | tf_op jit(solution)/shard_map/ppermute | solution.py:27
  101.5 10.3 %collective-permute-start.17 = (bf16[2,144,768]{2,1,0:T(8,128)(2,1)S(1)}, bf16[2,144,768]{2,1,0:T(8,128)(2,1)S(1)}, u32[]{:S(2)}, u32[]{:S(2)}) collective-permute-start(bf16[2,144,768]{2,1,0:T(8,128)(2,1)S(1)} %get-tuple-element.74), channel_id=1, source_target_pairs={{0,6},{1,193},{2,0},{3,195},{4,2},{5,197},{6,4},{7,199},{64,70},{6... | collective-permute-start | bytes 1327112 | tf_op jit(solution)/shard_map/ppermute | solution.py:27
  112.1 6.4 %collective-permute-start.18 = (bf16[144,768]{1,0:T(8,128)(2,1)S(1)}, bf16[144,768]{1,0:T(8,128)(2,1)S(1)}, u32[]{:S(2)}, u32[]{:S(2)}) collective-permute-start(bf16[144,768]{1,0:T(8,128)(2,1)S(1)} %get-tuple-element.82), channel_id=1, source_target_pairs={{0,64},{1,3},{2,66},{3,5},{4,68},{5,7},{6,70},{7,1},{64,128},{65,6... | collective-permute-start | bytes 663560 | tf_op jit(solution)/shard_map/ppermute | solution.py:27
  112.4 9.5 %collective-permute-start.19 = (bf16[144,768]{1,0:T(8,128)(2,1)S(1)}, bf16[144,768]{1,0:T(8,128)(2,1)S(1)}, u32[]{:S(2)}, u32[]{:S(2)}) collective-permute-start(bf16[144,768]{1,0:T(8,128)(2,1)S(1)} %get-tuple-element.81), channel_id=1, source_target_pairs={{0,128},{1,5},{2,130},{3,7},{4,132},{5,1},{6,134},{7,3},{64,192},{... | collective-permute-start | bytes 663560 | tf_op jit(solution)/shard_map/ppermute | solution.py:27
  116.0 18.1 %copy-start.3 = (bf16[320,128]{1,0:T(8,128)(2,1)S(1)}, bf16[320,128]{1,0:T(8,128)(2,1)}, u32[]{:S(2)}) copy-start(bf16[320,128]{1,0:T(8,128)(2,1)} %get-tuple-element.38.pick) | copy-start | bytes 245764
  116.0 5.9 %collective-permute-start.20 = (bf16[144,768]{1,0:T(8,128)(2,1)S(1)}, bf16[144,768]{1,0:T(8,128)(2,1)S(1)}, u32[]{:S(2)}, u32[]{:S(2)}) collective-permute-start(bf16[144,768]{1,0:T(8,128)(2,1)S(1)} %get-tuple-element.80), channel_id=1, source_target_pairs={{0,192},{1,7},{2,194},{3,1},{4,196},{5,3},{6,198},{7,5},{64,0},{65... | collective-permute-start | bytes 663560 | tf_op jit(solution)/shard_map/ppermute | solution.py:27
  134.4 4.7 %collective-permute-start.22 = (f32[128,384]{1,0:T(8,128)S(1)}, f32[128,384]{1,0:T(8,128)S(1)}, u32[]{:S(2)}, u32[]{:S(2)}) collective-permute-start(f32[128,384]{1,0:T(8,128)S(1)} %get-tuple-element.69), channel_id=1, source_target_pairs={{0,1},{1,0},{2,3},{3,2},{4,5},{5,4},{6,7},{7,6},{8,9},{9,8},{10,11... | collective-permute-start | bytes 589832 | tf_op jit(solution)/shard_map/ppermute | solution.py:15
where the time goes:
time: 140 us
  starting transfers between devices  36.9 us (26%)
  blocking collectives  35.7 us (26%)
  Pallas kernels  33.8 us (24%)
  waiting for transfers between devices  30.7 us (22%)
  other arithmetic  1.6 us (1%)
    all_to_all x2, blocking collectives, exchange(): a = lax.all_to_all(a, 'expert', split_axis=0, concat_axis=0, tiled=True)  35.7 us
    ppermute x18, waiting for transfers between devices, ring(): return lax.ppermute(a, ('dp', 'x', 'core'), pairs)  29.6 us
    pallas_call x9, Pallas kernels, call_inside(): pl.pallas_call(body, in_specs=[SCALARS] + [INSIDE] * (len(args) - 1), out...  28.3 us
    ppermute x18, starting transfers between devices, ring(): return lax.ppermute(a, ('dp', 'x', 'core'), pairs)  25.5 us
    ppermute x5, starting transfers between devices, swap(): return lax.ppermute(a, 'core', [(0, 1), (1, 0)])  11.4 us
    pallas_call x2, Pallas kernels, call(): pl.pallas_call(body, grid_spec=pltpu.PrefetchScalarGridSpec(num_scalar_pr...  5.48 us
  transfers between devices with their start and end apart: 23, of which 13 were waited for; matrix products, arithmetic and copies ran while one was open for 1% of the time, Pallas kernels for 18%

commit v1 on v0

--- a/solution.py
+++ b/solution.py
@@ -313,23 +313,25 @@
 
         @pl.when(core_of(xi) == 1)
         def _():
-            for k, (p, n) in enumerate(last):
-                hu2 = dot(p[n, :rows], w[2], ((1,), (0,)))
-                finish(k, hu2, dot(p[n, rows:], wd[2], ((1,), (1,))))
-
-        @pl.loop(0, 4)
-        def _(k):
-            out = dot(g[...], w[k], ((1,), (1,))).astype(BF)
-
-            @pl.when(core_of(xi) == 0)
-            def _():
-                for j in range(4):
-                    keep[k, j] = out[j * rows : (j + 1) * rows]
-
-            @pl.when(core_of(xi) == 1)
-            def _():
-                for j in range(4):
-                    keep[j, k] = out[j * rows : (j + 1) * rows]
+            x = jnp.concatenate([p[n, :rows] for p, n in last], axis=0)
+            y = jnp.concatenate([p[n, rows:] for p, n in last], axis=0)
+            hu2 = dot(x, w[2], ((1,), (0,)))
+            ga2 = dot(y, wd[2], ((1,), (1,)))
+            for k in range(4):
+                r = slice(k * rows, (k + 1) * rows)
+                finish(k, hu2[r], ga2[r])
+
+        @pl.when(core_of(xi) == 0)
+        def _():
+            out = dot(g[...], w[2], ((1,), (1,))).astype(BF)
+            for j in range(4):
+                keep[j] = out[j * rows : (j + 1) * rows]
+
+        @pl.when(core_of(xi) == 1)
+        def _():
+            mine = g[2 * rows : 3 * rows]
+            for k in range(4):
+                keep[k] = dot(mine, w[k], ((1,), (1,))).astype(BF)
 
     return call_inside(
         body,
@@ -337,28 +339,64 @@
         [
             jax.ShapeDtypeStruct((every, 2 * hid), BF),
             jax.ShapeDtypeStruct((every, 4 * hid), BF),
-            jax.ShapeDtypeStruct((4, 4, rows, cols), BF),
+            jax.ShapeDtypeStruct((4, rows, cols), BF),
         ],
         (at, hu, ga, p2a, p2b, w, wd),
-        2 * every * 4 * cols * 4 * hid,
+        every * 4 * cols * 4 * hid,
         20,
     )
 
 
-def weight_part(at, pieces, act, g, which, dtype):
+def other_blocks(at, g, w):
+    cols = w.shape[1]
+    rows = g.shape[0] // 4
+    places = (0, 1, 3)
+
+    def body(xi, g, w, keep):
+        @pl.when(core_of(xi) == 0)
+        def _():
+            for n, k in enumerate(places):
+                out = dot(g[...], w[k], ((1,), (1,))).astype(BF)
+                for j in range(4):
+                    keep[n, j] = out[j * rows : (j + 1) * rows]
+
+        @pl.when(core_of(xi) == 1)
+        def _():
+            mine = jnp.concatenate([g[: 2 * rows], g[3 * rows :]], axis=0)
+
+            @pl.loop(0, 4)
+            def _(k):
+                out = dot(mine, w[k], ((1,), (1,))).astype(BF)
+                for n in range(3):
+                    keep[n, k] = out[n * rows : (n + 1) * rows]
+
+    return call_inside(
+        body,
+        INSIDE,
+        jax.ShapeDtypeStruct((3, 4, rows, cols), BF),
+        (at, g, w),
+        2 * 3 * rows * 4 * cols * w.shape[2],
+        12,
+    )
+
+
+def weight_part(at, pieces, act, g, which, dtype, up=True, down=True):
     p0 = pieces[0]
     rows, cols = p0.shape[1] // 2, p0.shape[2]
     every, width = 4 * rows, 4 * cols
     hid = act.shape[1] // 2
     squares = [slice(j * hid, (j + 1) * hid) for j in range(cols // hid)]
+    size = (2 * up + down) * hid
 
     def body(xi, p0, p1a, p1b, p2a, p2b, p3a, p3b, act, g, *refs):
         xbuf, ybuf = refs[-2:]
 
         def load(sources):
             for j, (ref, n) in enumerate(sources):
-                xbuf[j * rows : (j + 1) * rows] = ref[n, :rows]
-                ybuf[j * rows : (j + 1) * rows] = ref[n, rows:]
+                if up:
+                    xbuf[j * rows : (j + 1) * rows] = ref[n, :rows]
+                if down:
+                    ybuf[j * rows : (j + 1) * rows] = ref[n, rows:]
 
         def step(k):
             on0 = core_of(xi) == 0
@@ -381,36 +419,38 @@
             cut = slice(which * hid, (which + 1) * hid)
             cut2 = slice(2 * which * hid, 2 * (which + 1) * hid)
             return (
-                dot(xbuf[...], g[:, cut2], ((0,), (0,))),
-                dot(act[:, cut], ybuf[...], ((0,), (0,))),
+                dot(xbuf[...], g[:, cut2], ((0,), (0,))) if up else None,
+                dot(act[:, cut], ybuf[...], ((0,), (0,))) if down else None,
             )
 
         out = refs[0]
 
         @pl.loop(0, 4)
         def _(k):
-            up, down = step(k)
-            out[k, :, : 2 * hid] = up.astype(out.dtype)
-            for c in squares:
-                out[k, c, 2 * hid :] = down[:, c].astype(out.dtype)
+            for_up, for_down = step(k)
+            if up:
+                out[k, :, : 2 * hid] = for_up.astype(out.dtype)
+            if down:
+                for c in squares:
+                    out[k, c, size - hid :] = for_down[:, c].astype(out.dtype)
 
     return call_inside(
         body,
         INSIDE,
-        jax.ShapeDtypeStruct((4, cols, 3 * hid), dtype),
+        jax.ShapeDtypeStruct((4, cols, size), dtype),
         (at, *pieces, act, g),
-        2 * 3 * every * width * hid,
+        2 * every * width * size,
         14,
         [pltpu.VMEM((every, cols), BF)] * 2,
     )
 
 
-def weight_sum(at, mine, other):
+def weight_sum(at, mine, other_up, other_down):
     _, cols, hid = mine.shape
     hid //= 3
     width = 4 * cols
 
-    def body(xi, mine, other, og, ou, od, sg, su, sd, sems):
+    def body(xi, mine, up, down, og, ou, od, sg, su, sd, sems):
         def copies(k):
             block = pl.ds(pl.multiple_of((x_of(xi) + k) % 4 * cols, cols), cols)
             return (
@@ -421,12 +461,13 @@
 
         @pl.loop(0, 4)
         def _(k):
-            total = (mine[k] + other[k].astype(F32)).astype(BF)
+            total = (mine[k, :, : 2 * hid] + up[k].astype(F32)).astype(BF)
             sg[k] = total[:, :hid]
-            su[k] = total[:, hid : 2 * hid]
+            su[k] = total[:, hid:]
+            total = (mine[k, :, 2 * hid :] + down[k].astype(F32)).astype(BF)
             for j in range(cols // hid):
                 c = slice(j * hid, (j + 1) * hid)
-                sd[k, :, c] = total[c, 2 * hid :]
+                sd[k, :, c] = total[c]
             for copy in copies(k):
                 copy.start()
 
@@ -443,7 +484,7 @@
             jax.ShapeDtypeStruct((width, hid), BF),
             jax.ShapeDtypeStruct((hid, width), BF),
         ],
-        (at, mine, other),
+        (at, mine, other_up, other_down),
         12 * width * hid,
         14,
         [
@@ -476,7 +517,8 @@
     got = compact(at, got, experts, half)
     w, wd = pack(at, own, theirs)
 
-    p0 = jnp.stack([got, ring(got, False, -1), ring(got, False, 2), ring(got, False, 1)])
+    f1, f3, f2 = ring(got, False, -1), ring(got, False, 1), ring(got, False, 2)
+    p0 = jnp.stack([got, f1, f2, f3])
     p1a, p3b = ring(p0[:2], True, -1), ring(p0[2:], True, 1)
     p1b, p3a = ring(p0[2:], True, -1), ring(p0[:2], True, 1)
     early = early_part(at, (p0,), ((0, 0),), w, wd)
@@ -485,21 +527,24 @@
     places = ((0, 1), (2, 1), (0, 3), (2, 3))
     hu, ga = early_part(at, (p1a, p1b, p3a, p3b), places, w, wd, early)
     p2a, p2b = tie((p2a, p2b), hu, ga)
-    act, g, keep = token_part(at, hu, ga, p2a, p2b, w, wd)
+    act, g, first = token_part(at, hu, ga, p2a, p2b, w, wd)
     pieces = (p0, p1a, p1b, p2a, p2b, p3a, p3b)
 
-    k_up, v_dn = ring(keep[2, :2], False, 1), ring(keep[2, 2:], False, -1)
-    part = weight_part(at, pieces, act, g, 1, BF)
+    k_up, v_dn = ring(first[:2], False, 1), ring(first[2:], False, -1)
+    keep = other_blocks(at, g, w)
+    part = weight_part(at, pieces, act, g, 1, BF, down=False)
     k_up, v_dn, part, keep = tie((k_up, v_dn, part, keep))
-    k_up, v_dn = tie((add(keep[1, :2], k_up), add(keep[3, 2:], v_dn)))
+    k_up, v_dn = tie((add(keep[1, :2], k_up), add(keep[2, 2:], v_dn)))
     k_up, v_dn = ring(k_up, False, 1), ring(v_dn, False, -1)
-    v_up, k_dn = ring(keep[1, 2:], False, 1), ring(keep[3, :2], False, -1)
+    v_up, k_dn = ring(keep[1, 2:], False, 1), ring(keep[2, :2], False, -1)
     part = swap(part)
     mine = weight_part(at, pieces, act, g, 0, F32)
-    k_up, v_dn, v_up, k_dn = tie((k_up, v_dn, v_up, k_dn), mine)
+    rest = weight_part(at, pieces, act, g, 1, BF, up=False)
+    k_up, v_dn, v_up, k_dn, rest = tie((k_up, v_dn, v_up, k_dn, rest), mine)
+    rest = swap(rest)
     total = jnp.concatenate([add(keep[0, :2], k_up, k_dn), add(keep[0, 2:], v_up, v_dn)], axis=0)
-    parts = [ring(total[k], True, k) for k in (1, 2, 3)]
-    gw_gate, gw_up, gw_down = weight_sum(at, mine, part)
+    parts = [ring(total[k], True, k) for k in (1, 3, 2)]
+    gw_gate, gw_up, gw_down = weight_sum(at, mine, part, rest)
     parts = tie(parts, gw_gate)
 
     back = exchange(spread(at, [total[0], *parts], experts, slots))

time: 140 us -> 138 us (0.986)
  starting transfers between devices: 36.9 us -> 34.1 us
  Pallas kernels: 33.8 us -> 35.4 us
    ppermute x18, starting transfers between devices: 25.5 us -> 22.6 us  [ring(): return lax.ppermute(a, ('dp', 'x', 'core'), pairs)]
    pallas_call x9 -> x11, Pallas kernels: 28.3 us -> 29.9 us  [call_inside(): pl.pallas_call(body, in_specs=[SCALARS] + [INSIDE] * (len(args) - 1), out...]
    ppermute x5 -> x6, starting transfers between devices: 11.4 us -> 11.4 us  [swap(): return lax.ppermute(a, 'core', [(0, 1), (1, 0)])]
  transfers between devices with their start and end apart: 23 -> 24, of which waited for: 13 -> 13; matrix products, arithmetic and copies ran while one was open for 1% -> 1% of each run, Pallas kernels for 18% -> 22%
where the time goes in v1:
time: 138 us
  Pallas kernels  35.4 us (26%)
  blocking collectives  35.3 us (26%)
  starting transfers between devices  34.1 us (25%)
  waiting for transfers between devices  30.5 us (22%)
  other arithmetic  1.61 us (1%)
    all_to_all x2, blocking collectives, exchange(): a = lax.all_to_all(a, 'expert', split_axis=0, concat_axis=0, tiled=True)  35.3 us
    pallas_call x11, Pallas kernels, call_inside(): pl.pallas_call(body, in_specs=[SCALARS] + [INSIDE] * (len(args) - 1), out...  29.9 us
    ppermute x18, waiting for transfers between devices, ring(): return lax.ppermute(a, ('dp', 'x', 'core'), pairs)  29.4 us
    ppermute x18, starting transfers between devices, ring(): return lax.ppermute(a, ('dp', 'x', 'core'), pairs)  22.6 us
    ppermute x6, starting transfers between devices, swap(): return lax.ppermute(a, 'core', [(0, 1), (1, 0)])  11.4 us
    pallas_call x2, Pallas kernels, call(): pl.pallas_call(body, grid_spec=pltpu.PrefetchScalarGridSpec(num_scalar_pr...  5.48 us
  transfers between devices with their start and end apart: 24, of which 13 were waited for; matrix products, arithmetic and copies ran while one was open for 1% of the time, Pallas kernels for 22%

profile of v1, /device:TPU:1, one launch (start us, length us, event | category | flops | bytes accessed | tf_op | source)
XLA Modules:
  0.0 137.9 jit_solution(204445338441357268)
XLA Ops:
  0.6 3.3 %collective-permute-start = (bf16[3072,256]{1,0:T(8,128)(2,1)}, bf16[3072,256]{1,0:T(8,128)(2,1)S(1)}, u32[]{:S(2)}, u32[]{:S(2)}) collective-permute-start(bf16[3072,256]{1,0:T(8,128)(2,1)} %bitcast.44), channel_id=1, source_target_pairs={{0,1},{1,0},{2,3},{3,2},{4,5},{5,4},{6,7},{7,6},{8,9},{9,8},{10,11... | collective-permute-start | bytes 4718600 | tf_op jit(solution)/shard_map/ppermute | solution.py:15
  4.1 0.4 collective-permute-start.2
  4.5 2.4 %shard_map.102 = (bf16[320,768]{1,0:T(8,128)(2,1)}, bf16[320,128]{1,0:T(8,128)(2,1)}) custom-call(s32[1]{0:T(128)} %bitcast.xi, s32[2,128]{1,0:T(2,128)} %bitcast.59, f32[2,128]{1,0:T(2,128)} %bitcast.60, bf16[128,3072]{1,0:T(8,128)(2,1)} %tok.1, bf16[128,3072]{1,0:T(8,128)(2,1)} %grad.1), custom_call_target="tpu_custom_call" | custom-call | flops 125829120 | bytes 8388608 | tf_op jit(solution)/shard_map/pallas_call | solution.py:51
  6.8 23.9 %all_to_all.10 = bf16[8,40,768]{2,1,0:T(8,128)(2,1)S(1)} all-to-all(bf16[8,40,768]{2,1,0:T(8,128)(2,1)} %bitcast.58), channel_id=1, replica_groups=mesh['dp'=4,'expert'=8,'x'=4,'core'=2] {'expert'}, dimensions={0} | all-to-all | bytes 983040 | tf_op jit(solution)/shard_map/all_to_all | solution.py:512
  30.7 0.4 shard_map.103
  31.1 1.4 collective-permute-start.6
  32.5 2.6 %collective-permute-start.5 = (bf16[288,768]{1,0:T(8,128)(2,1)S(1)}, bf16[288,768]{1,0:T(8,128)(2,1)S(1)}, u32[]{:S(2)}, u32[]{:S(2)}) collective-permute-start(bf16[288,768]{1,0:T(8,128)(2,1)S(1)} %shard_map.103), channel_id=1, source_target_pairs={{0,4},{1,129},{2,6},{3,131},{4,0},{5,133},{6,2},{7,135},{64,68},{6... | collective-permute-start | bytes 1327112 | tf_op jit(solution)/shard_map/ppermute | solution.py:27
  35.1 1.1 collective-permute-start.3
  36.2 3.7 %collective-permute-done.6 = bf16[288,768]{1,0:T(8,128)(2,1)S(1)} collective-permute-done((bf16[288,768]{1,0:T(8,128)(2,1)S(1)}, bf16[288,768]{1,0:T(8,128)(2,1)S(1)}, u32[]{:S(2)}, u32[]{:S(2)}) %collective-permute-start.6) | collective-permute-done | bytes 442400 | tf_op jit(solution)/shard_map/ppermute | solution.py:27
  39.9 5.9 %collective-permute-done.5 = bf16[288,768]{1,0:T(8,128)(2,1)S(1)} collective-permute-done((bf16[288,768]{1,0:T(8,128)(2,1)S(1)}, bf16[288,768]{1,0:T(8,128)(2,1)S(1)}, u32[]{:S(2)}, u32[]{:S(2)}) %collective-permute-start.5) | collective-permute-done | bytes 442400 | tf_op jit(solution)/shard_map/ppermute | solution.py:27
  45.9 1.0 collective-permute-start.7
  47.0 1.8 %collective-permute-start.4 = (bf16[2,288,768]{2,1,0:T(8,128)(2,1)S(1)}, bf16[2,288,768]{2,1,0:T(8,128)(2,1)S(1)}, u32[]{:S(2)}, u32[]{:S(2)}) collective-permute-start(bf16[2,288,768]{2,1,0:T(8,128)(2,1)S(1)} %pad_maximum_fusion.1), channel_id=1, source_target_pairs={{0,192},{1,7},{2,194},{3,1},{4,196},{5,3},{6,198},{7,5},{64,0},{65... | collective-permute-start | bytes 2654216 | tf_op jit(solution)/shard_map/ppermute | solution.py:27
  48.8 3.1 %shard_map.104 = (bf16[4,768,1024]{2,1,0:T(8,128)(2,1)S(1)}, bf16[4,512,768]{2,1,0:T(8,128)(2,1)S(1)}) custom-call(s32[1]{0:T(128)} %bitcast.xi, bf16[3072,256]{1,0:T(8,128)(2,1)S(1)} %bitcast.45, bf16[3072,256]{1,0:T(8,128)(2,1)S(1)} %bitcast.47, bf16[256,3072]{1,0:T(8,128)(2,1)S(1)} %bitcast.49, bf16[3072,256]{1,0:T(8,128)(2,1)S(1)} %collective-permute-done.g2, ...), custom_call_target="tpu_custom_call" | custom-call | flops 786432 | bytes 8388608 | tf_op jit(solution)/shard_map/pallas_call | solution.py:51
  52.0 1.1 collective-permute-start.8
  53.1 0.5 collective-permute-start.9
  53.7 2.9 %shard_map.105 = (f32[4,144,1024]{2,1,0:T(8,128)S(1)}, f32[4,144,512]{2,1,0:T(8,128)S(1)}) custom-call(s32[1]{0:T(128)} %bitcast.xi, bf16[4,288,768]{2,1,0:T(8,128)(2,1)S(1)} %pad_maximum_fusion.refs_0_.p0, bf16[4,768,1024]{2,1,0:T(8,128)(2,1)S(1)} %get-tuple-element.42.refs_1_.refs_4_.w, bf16[4,512,768]{2,1,0:T(8,128)(2,1)S(1)} %get-tuple-element.43.refs_2_.refs_5_.wd), custom_call_target="tpu_custom_call" | custom-call | flops 1358954496 | bytes 8388608 | tf_op jit(solution)/shard_map/pallas_call | solution.py:65
  56.6 2.8 %collective-permute-done.7.refs_3_.p3b = bf16[2,288,768]{2,1,0:T(8,128)(2,1)S(1)} collective-permute-done((bf16[2,288,768]{2,1,0:T(8,128)(2,1)S(1)}, bf16[2,288,768]{2,1,0:T(8,128)(2,1)S(1)}, u32[]{:S(2)}, u32[]{:S(2)}) %collective-permute-start.7) | collective-permute-done | bytes 884768 | tf_op jit(solution)/shard_map/ppermute | solution.py:27
  59.4 2.8 %collective-permute-start.10 = (bf16[2,288,768]{2,1,0:T(8,128)(2,1)S(1)}, bf16[2,288,768]{2,1,0:T(8,128)(2,1)S(1)}, u32[]{:S(2)}, u32[]{:S(2)}) collective-permute-start(bf16[2,288,768]{2,1,0:T(8,128)(2,1)S(1)} %collective-permute-done.4.refs_0_.p1a), channel_id=1, source_target_pairs={{0,192},{1,7},{2,194},{3,1},{4,196},{5,3},{6,198},{7,5},{64,0},{65... | collective-permute-start | bytes 2654216 | tf_op jit(solution)/shard_map/ppermute | solution.py:27
  62.2 6.5 %collective-permute-done.8.refs_1_.p1b = bf16[2,288,768]{2,1,0:T(8,128)(2,1)S(1)} collective-permute-done((bf16[2,288,768]{2,1,0:T(8,128)(2,1)S(1)}, bf16[2,288,768]{2,1,0:T(8,128)(2,1)S(1)}, u32[]{:S(2)}, u32[]{:S(2)}) %collective-permute-start.8) | collective-permute-done | bytes 884768 | tf_op jit(solution)/shard_map/ppermute | solution.py:27
  68.9 4.5 %shard_map.106 = (f32[4,144,1024]{2,1,0:T(8,128)S(1)}, f32[4,144,512]{2,1,0:T(8,128)S(1)}) custom-call(s32[1]{0:T(128)} %bitcast.xi, bf16[2,288,768]{2,1,0:T(8,128)(2,1)S(1)} %collective-permute-done.4.refs_0_.p1a, bf16[2,288,768]{2,1,0:T(8,128)(2,1)S(1)} %collective-permute-done.8.refs_1_.p1b, bf16[2,288,768]{2,1,0:T(8,128)(2,1)S(1)} %collective-permute-done.9.refs_2_.p3a, ...), custom_call_target="tpu_custom_call" | custom-call | flops 2717908992 | bytes 8388608 | tf_op jit(solution)/shard_map/pallas_call | solution.py:65
  73.4 4.8 %collective-permute-done.10.pa.p2a = bf16[2,288,768]{2,1,0:T(8,128)(2,1)S(1)} collective-permute-done((bf16[2,288,768]{2,1,0:T(8,128)(2,1)S(1)}, bf16[2,288,768]{2,1,0:T(8,128)(2,1)S(1)}, u32[]{:S(2)}, u32[]{:S(2)}) %collective-permute-start.10) | collective-permute-done | bytes 884768 | tf_op jit(solution)/shard_map/ppermute | solution.py:27
  78.4 4.1 %shard_map.107 = (bf16[576,512]{1,0:T(8,128)(2,1)S(1)}, bf16[576,1024]{1,0:T(8,128)(2,1)S(1)}, bf16[4,144,768]{2,1,0:T(8,128)(2,1)S(1)}) custom-call(s32[1]{0:T(128)} %bitcast.xi, f32[4,144,1024]{2,1,0:T(8,128)S(1)} %get-tuple-element.48.hu, f32[4,144,512]{2,1,0:T(8,128)S(1)} %get-tuple-element.49.ga, ...), custom_call_target="tpu_custom_call" | custom-call | flops 1811939328 | bytes 8388608 | tf_op jit(solution)/shard_map/pallas_call | solution.py:65
  82.5 1.0 collective-permute-start.13
  83.5 0.5 collective-permute-start.12
  84.0 3.6 %shard_map.108 = bf16[4,768,512]{2,1,0:T(8,128)(2,1)S(1)} custom-call(s32[1]{0:T(128)} %bitcast.xi, bf16[4,288,768]{2,1,0:T(8,128)(2,1)S(1)} %pad_maximum_fusion.refs_0_.p0, bf16[2,288,768]{2,1,0:T(8,128)(2,1)S(1)} %collective-permute-done.4.refs_0_.p1a, bf16[2,288,768]{2,1,0:T(8,128)(2,1)S(1)} %collective-permute-done.8.refs_1_.p1b, ...), custom_call_target="tpu_custom_call" | custom-call | flops 1811939328 | bytes 8388608 | tf_op jit(solution)/shard_map/pallas_call | solution.py:65
  87.6 3.9 %shard_map.109 = bf16[3,4,144,768]{3,2,1,0:T(8,128)(2,1)S(1)} custom-call(s32[1]{0:T(128)} %bitcast.xi, bf16[576,1024]{1,0:T(8,128)(2,1)S(1)} %get-tuple-element.54.g, bf16[4,768,1024]{2,1,0:T(8,128)(2,1)S(1)} %get-tuple-element.42.refs_1_.refs_4_.w), custom_call_target="tpu_custom_call" | custom-call | flops 2717908992 | bytes 8388608 | tf_op jit(solution)/shard_map/pallas_call | solution.py:65
  91.5 0.7 collective-permute-done.12
  92.2 3.6 %collective-permute-start.21 = (bf16[4,768,512]{2,1,0:T(8,128)(2,1)S(1)}, bf16[4,768,512]{2,1,0:T(8,128)(2,1)S(1)}, u32[]{:S(2)}, u32[]{:S(2)}) collective-permute-start(bf16[4,768,512]{2,1,0:T(8,128)(2,1)S(1)} %shard_map.108), channel_id=1, source_target_pairs={{0,1},{1,0},{2,3},{3,2},{4,5},{5,4},{6,7},{7,6},{8,9},{9,8},{10,11... | collective-permute-start | bytes 9437192 | tf_op jit(solution)/shard_map/ppermute | solution.py:15
  96.0 0.8 collective-permute-start.14
  96.8 2.7 %collective-permute-start.15 = (bf16[2,144,768]{2,1,0:T(8,128)(2,1)S(1)}, bf16[2,144,768]{2,1,0:T(8,128)(2,1)S(1)}, u32[]{:S(2)}, u32[]{:S(2)}) collective-permute-start(bf16[2,144,768]{2,1,0:T(8,128)(2,1)S(1)} %get-tuple-element.59), channel_id=1, source_target_pairs={{0,6},{1,193},{2,0},{3,195},{4,2},{5,197},{6,4},{7,199},{64,70},{6... | collective-permute-start | bytes 1327112 | tf_op jit(solution)/shard_map/ppermute | solution.py:27
  99.6 1.5 %collective-permute-start.17 = (bf16[2,144,768]{2,1,0:T(8,128)(2,1)S(1)}, bf16[2,144,768]{2,1,0:T(8,128)(2,1)S(1)}, u32[]{:S(2)}, u32[]{:S(2)}) collective-permute-start(bf16[2,144,768]{2,1,0:T(8,128)(2,1)S(1)} %get-tuple-element.76), channel_id=1, source_target_pairs={{0,6},{1,193},{2,0},{3,195},{4,2},{5,197},{6,4},{7,199},{64,70},{6... | collective-permute-start | bytes 1327112 | tf_op jit(solution)/shard_map/ppermute | solution.py:27
  101.2 2.4 %shard_map.110 = bf16[4,768,256]{2,1,0:T(8,128)(2,1)S(1)} custom-call(s32[1]{0:T(128)} %bitcast.xi, bf16[4,288,768]{2,1,0:T(8,128)(2,1)S(1)} %pad_maximum_fusion.refs_0_.p0, bf16[2,288,768]{2,1,0:T(8,128)(2,1)S(1)} %collective-permute-done.4.refs_0_.p1a, bf16[2,288,768]{2,1,0:T(8,128)(2,1)S(1)} %collective-permute-done.8.refs_1_.p1b, ...), custom_call_target="tpu_custom_call" | custom-call | flops 905969664 | bytes 8388608 | tf_op jit(solution)/shard_map/pallas_call | solution.py:65
  103.6 5.2 %shard_map.111.mine = f32[4,768,768]{2,1,0:T(8,128)S(1)} custom-call(s32[1]{0:T(128)} %bitcast.xi, bf16[4,288,768]{2,1,0:T(8,128)(2,1)S(1)} %pad_maximum_fusion.refs_0_.p0, bf16[2,288,768]{2,1,0:T(8,128)(2,1)S(1)} %collective-permute-done.4.refs_0_.p1a, bf16[2,288,768]{2,1,0:T(8,128)(2,1)S(1)} %collective-permute-done.8.refs_1_.p1b, ...), custom_call_target="tpu_custom_call" | custom-call | flops 2717908992 | bytes 8388608 | tf_op jit(solution)/shard_map/pallas_call | solution.py:65
  108.8 0.8 collective-permute-done.17
  109.6 0.4 collective-permute-done.16
  109.9 0.4 collective-permute-start.22
  110.3 0.3 fusion.1
  110.7 1.3 collective-permute-start.20
  112.0 1.9 %collective-permute-start.19 = (bf16[144,768]{1,0:T(8,128)(2,1)S(1)}, bf16[144,768]{1,0:T(8,128)(2,1)S(1)}, u32[]{:S(2)}, u32[]{:S(2)}) collective-permute-start(bf16[144,768]{1,0:T(8,128)(2,1)S(1)} %get-tuple-element.83), channel_id=1, source_target_pairs={{0,192},{1,7},{2,194},{3,1},{4,196},{5,3},{6,198},{7,5},{64,0},{65... | collective-permute-start | bytes 663560 | tf_op jit(solution)/shard_map/ppermute | solution.py:27
  113.9 0.6 collective-permute-start.18
  114.5 2.3 %shard_map.112 = (bf16[3072,256]{1,0:T(8,128)(2,1)}, bf16[3072,256]{1,0:T(8,128)(2,1)}, bf16[256,3072]{1,0:T(8,128)(2,1)}) custom-call(s32[1]{0:T(128)} %bitcast.xi, f32[4,768,768]{2,1,0:T(8,128)S(1)} %shard_map.111.mine, bf16[4,768,512]{2,1,0:T(8,128)(2,1)S(1)} %collective-permute-done.21.up, bf16[4,768,256]{2,1,0:T(8,128)(2,1)S(1)} %collective-permute-done.22.down), custom_call_target="tpu_custom_call" | custom-call | flops 9437184 | bytes 8388608 | tf_op jit(solution)/shard_map/pallas_call | solution.py:65
  116.8 0.6 collective-permute-done.20.refs_3_
  117.4 3.0 %collective-permute-done.19.refs_2_ = bf16[144,768]{1,0:T(8,128)(2,1)S(1)} collective-permute-done((bf16[144,768]{1,0:T(8,128)(2,1)S(1)}, bf16[144,768]{1,0:T(8,128)(2,1)S(1)}, u32[]{:S(2)}, u32[]{:S(2)}) %collective-permute-start.19) | collective-permute-done | bytes 221216 | tf_op jit(solution)/shard_map/ppermute | solution.py:27
  120.4 0.4 shard_map.113
  120.8 11.4 %all_to_all.11 = bf16[8,40,384]{2,1,0:T(8,128)(2,1)S(1)} all-to-all(bf16[8,40,384]{2,1,0:T(8,128)(2,1)S(1)} %bitcast.51), channel_id=1, replica_groups=mesh['dp'=4,'expert'=8,'x'=4,'core'=2] {'expert'}, dimensions={0} | all-to-all | bytes 491520 | tf_op jit(solution)/shard_map/all_to_all | solution.py:512
  132.5 3.6 %collective-permute-start.23 = (f32[128,384]{1,0:T(8,128)S(1)}, f32[128,384]{1,0:T(8,128)S(1)}, u32[]{:S(2)}, u32[]{:S(2)}) collective-permute-start(f32[128,384]{1,0:T(8,128)S(1)} %get-tuple-element.71), channel_id=1, source_target_pairs={{0,1},{1,0},{2,3},{3,2},{4,5},{5,4},{6,7},{7,6},{8,9},{9,8},{10,11... | collective-permute-start | bytes 589832 | tf_op jit(solution)/shard_map/ppermute | solution.py:15
  136.1 1.1 collective-permute-done.23
  137.2 0.7 add_convert_fusion
  (33 shorter events, 1.6 us)
Async XLA Ops:
  0.6 30.1 %collective-permute-start = (bf16[3072,256]{1,0:T(8,128)(2,1)}, bf16[3072,256]{1,0:T(8,128)(2,1)S(1)}, u32[]{:S(2)}, u32[]{:S(2)}) collective-permute-start(bf16[3072,256]{1,0:T(8,128)(2,1)} %bitcast.44), channel_id=1, source_target_pairs={{0,1},{1,0},{2,3},{3,2},{4,5},{5,4},{6,7},{7,6},{8,9},{9,8},{10,11... | collective-permute-start | bytes 4718600 | tf_op jit(solution)/shard_map/ppermute | solution.py:15
  4.0 26.8 %collective-permute-start.1 = (bf16[3072,256]{1,0:T(8,128)(2,1)}, bf16[3072,256]{1,0:T(8,128)(2,1)S(1)}, u32[]{:S(2)}, u32[]{:S(2)}) collective-permute-start(bf16[3072,256]{1,0:T(8,128)(2,1)} %bitcast.46), channel_id=1, source_target_pairs={{0,1},{1,0},{2,3},{3,2},{4,5},{5,4},{6,7},{7,6},{8,9},{9,8},{10,11... | collective-permute-start | bytes 4718600 | tf_op jit(solution)/shard_map/ppermute | solution.py:15
  4.1 26.7 %collective-permute-start.2 = (bf16[256,3072]{1,0:T(8,128)(2,1)}, bf16[256,3072]{1,0:T(8,128)(2,1)}, u32[]{:S(2)}, u32[]{:S(2)}) collective-permute-start(bf16[256,3072]{1,0:T(8,128)(2,1)} %bitcast.48), channel_id=1, source_target_pairs={{0,1},{1,0},{2,3},{3,2},{4,5},{5,4},{6,7},{7,6},{8,9},{9,8},{10,11... | collective-permute-start | bytes 4718600 | tf_op jit(solution)/shard_map/ppermute | solution.py:15
  6.8 42.0 %copy-start.2 = (bf16[1,256,3072]{2,1,0:T(8,128)(2,1)S(1)}, bf16[1,256,3072]{2,1,0:T(8,128)(2,1)}, u32[]{:S(2)}) copy-start(bf16[1,256,3072]{2,1,0:T(8,128)(2,1)} %param.13) | copy-start | bytes 4718596
  31.1 8.8 %collective-permute-start.6 = (bf16[288,768]{1,0:T(8,128)(2,1)S(1)}, bf16[288,768]{1,0:T(8,128)(2,1)S(1)}, u32[]{:S(2)}, u32[]{:S(2)}) collective-permute-start(bf16[288,768]{1,0:T(8,128)(2,1)S(1)} %shard_map.103), channel_id=1, source_target_pairs={{0,2},{1,65},{2,4},{3,67},{4,6},{5,69},{6,0},{7,71},{64,66},{65,12... | collective-permute-start | bytes 1327112 | tf_op jit(solution)/shard_map/ppermute | solution.py:27
  32.5 13.3 %collective-permute-start.5 = (bf16[288,768]{1,0:T(8,128)(2,1)S(1)}, bf16[288,768]{1,0:T(8,128)(2,1)S(1)}, u32[]{:S(2)}, u32[]{:S(2)}) collective-permute-start(bf16[288,768]{1,0:T(8,128)(2,1)S(1)} %shard_map.103), channel_id=1, source_target_pairs={{0,4},{1,129},{2,6},{3,131},{4,0},{5,133},{6,2},{7,135},{64,68},{6... | collective-permute-start | bytes 1327112 | tf_op jit(solution)/shard_map/ppermute | solution.py:27
  35.1 11.8 %collective-permute-start.3 = (bf16[288,768]{1,0:T(8,128)(2,1)S(1)}, bf16[288,768]{1,0:T(8,128)(2,1)S(1)}, u32[]{:S(2)}, u32[]{:S(2)}) collective-permute-start(bf16[288,768]{1,0:T(8,128)(2,1)S(1)} %shard_map.103), channel_id=1, source_target_pairs={{0,6},{1,193},{2,0},{3,195},{4,2},{5,197},{6,4},{7,199},{64,70},{6... | collective-permute-start | bytes 1327112 | tf_op jit(solution)/shard_map/ppermute | solution.py:27
  45.8 3.0 %copy-start = (bf16[1,3072,256]{2,1,0:T(8,128)(2,1)S(1)}, bf16[1,3072,256]{2,1,0:T(8,128)(2,1)}, u32[]{:S(2)}) copy-start(bf16[1,3072,256]{2,1,0:T(8,128)(2,1)} %param.11) | copy-start | bytes 4718596
  45.8 3.0 %copy-start.1 = (bf16[1,3072,256]{2,1,0:T(8,128)(2,1)S(1)}, bf16[1,3072,256]{2,1,0:T(8,128)(2,1)}, u32[]{:S(2)}) copy-start(bf16[1,3072,256]{2,1,0:T(8,128)(2,1)} %param.12) | copy-start | bytes 4718596
  45.9 13.5 %collective-permute-start.7 = (bf16[2,288,768]{2,1,0:T(8,128)(2,1)S(1)}, bf16[2,288,768]{2,1,0:T(8,128)(2,1)S(1)}, u32[]{:S(2)}, u32[]{:S(2)}) collective-permute-start(bf16[2,288,768]{2,1,0:T(8,128)(2,1)S(1)} %pad_maximum_fusion.2), channel_id=1, source_target_pairs={{0,64},{1,3},{2,66},{3,5},{4,68},{5,7},{6,70},{7,1},{64,128},{65,6... | collective-permute-start | bytes 2654216 | tf_op jit(solution)/shard_map/ppermute | solution.py:27
  47.0 12.4 %collective-permute-start.4 = (bf16[2,288,768]{2,1,0:T(8,128)(2,1)S(1)}, bf16[2,288,768]{2,1,0:T(8,128)(2,1)S(1)}, u32[]{:S(2)}, u32[]{:S(2)}) collective-permute-start(bf16[2,288,768]{2,1,0:T(8,128)(2,1)S(1)} %pad_maximum_fusion.1), channel_id=1, source_target_pairs={{0,192},{1,7},{2,194},{3,1},{4,196},{5,3},{6,198},{7,5},{64,0},{65... | collective-permute-start | bytes 2654216 | tf_op jit(solution)/shard_map/ppermute | solution.py:27
  52.0 16.8 %collective-permute-start.8 = (bf16[2,288,768]{2,1,0:T(8,128)(2,1)S(1)}, bf16[2,288,768]{2,1,0:T(8,128)(2,1)S(1)}, u32[]{:S(2)}, u32[]{:S(2)}) collective-permute-start(bf16[2,288,768]{2,1,0:T(8,128)(2,1)S(1)} %pad_maximum_fusion.2), channel_id=1, source_target_pairs={{0,192},{1,7},{2,194},{3,1},{4,196},{5,3},{6,198},{7,5},{64,0},{65... | collective-permute-start | bytes 2654216 | tf_op jit(solution)/shard_map/ppermute | solution.py:27
  53.1 15.8 %collective-permute-start.9 = (bf16[2,288,768]{2,1,0:T(8,128)(2,1)S(1)}, bf16[2,288,768]{2,1,0:T(8,128)(2,1)S(1)}, u32[]{:S(2)}, u32[]{:S(2)}) collective-permute-start(bf16[2,288,768]{2,1,0:T(8,128)(2,1)S(1)} %pad_maximum_fusion.1), channel_id=1, source_target_pairs={{0,64},{1,3},{2,66},{3,5},{4,68},{5,7},{6,70},{7,1},{64,128},{65,6... | collective-permute-start | bytes 2654216 | tf_op jit(solution)/shard_map/ppermute | solution.py:27
  59.4 18.8 %collective-permute-start.10 = (bf16[2,288,768]{2,1,0:T(8,128)(2,1)S(1)}, bf16[2,288,768]{2,1,0:T(8,128)(2,1)S(1)}, u32[]{:S(2)}, u32[]{:S(2)}) collective-permute-start(bf16[2,288,768]{2,1,0:T(8,128)(2,1)S(1)} %collective-permute-done.4.refs_0_.p1a), channel_id=1, source_target_pairs={{0,192},{1,7},{2,194},{3,1},{4,196},{5,3},{6,198},{7,5},{64,0},{65... | collective-permute-start | bytes 2654216 | tf_op jit(solution)/shard_map/ppermute | solution.py:27
  62.2 16.1 %collective-permute-start.11 = (bf16[2,288,768]{2,1,0:T(8,128)(2,1)S(1)}, bf16[2,288,768]{2,1,0:T(8,128)(2,1)S(1)}, u32[]{:S(2)}, u32[]{:S(2)}) collective-permute-start(bf16[2,288,768]{2,1,0:T(8,128)(2,1)S(1)} %collective-permute-done.7.refs_3_.p3b), channel_id=1, source_target_pairs={{0,64},{1,3},{2,66},{3,5},{4,68},{5,7},{6,70},{7,1},{64,128},{65,6... | collective-permute-start | bytes 2654216 | tf_op jit(solution)/shard_map/ppermute | solution.py:27
  82.5 9.0 %collective-permute-start.13 = (bf16[2,144,768]{2,1,0:T(8,128)(2,1)S(1)}, bf16[2,144,768]{2,1,0:T(8,128)(2,1)S(1)}, u32[]{:S(2)}, u32[]{:S(2)}) collective-permute-start(bf16[2,144,768]{2,1,0:T(8,128)(2,1)S(1)} %get-tuple-element.80), channel_id=1, source_target_pairs={{0,6},{1,193},{2,0},{3,195},{4,2},{5,197},{6,4},{7,199},{64,70},{6... | collective-permute-start | bytes 1327112 | tf_op jit(solution)/shard_map/ppermute | solution.py:27
  83.5 8.7 %collective-permute-start.12 = (bf16[2,144,768]{2,1,0:T(8,128)(2,1)S(1)}, bf16[2,144,768]{2,1,0:T(8,128)(2,1)S(1)}, u32[]{:S(2)}, u32[]{:S(2)}) collective-permute-start(bf16[2,144,768]{2,1,0:T(8,128)(2,1)S(1)} %get-tuple-element.81), channel_id=1, source_target_pairs={{0,2},{1,65},{2,4},{3,67},{4,6},{5,69},{6,0},{7,71},{64,66},{65,12... | collective-permute-start | bytes 1327112 | tf_op jit(solution)/shard_map/ppermute | solution.py:27
  92.2 22.3 %collective-permute-start.21 = (bf16[4,768,512]{2,1,0:T(8,128)(2,1)S(1)}, bf16[4,768,512]{2,1,0:T(8,128)(2,1)S(1)}, u32[]{:S(2)}, u32[]{:S(2)}) collective-permute-start(bf16[4,768,512]{2,1,0:T(8,128)(2,1)S(1)} %shard_map.108), channel_id=1, source_target_pairs={{0,1},{1,0},{2,3},{3,2},{4,5},{5,4},{6,7},{7,6},{8,9},{9,8},{10,11... | collective-permute-start | bytes 9437192 | tf_op jit(solution)/shard_map/ppermute | solution.py:15
  96.0 12.8 %collective-permute-start.14 = (bf16[2,144,768]{2,1,0:T(8,128)(2,1)S(1)}, bf16[2,144,768]{2,1,0:T(8,128)(2,1)S(1)}, u32[]{:S(2)}, u32[]{:S(2)}) collective-permute-start(bf16[2,144,768]{2,1,0:T(8,128)(2,1)S(1)} %get-tuple-element.58), channel_id=1, source_target_pairs={{0,2},{1,65},{2,4},{3,67},{4,6},{5,69},{6,0},{7,71},{64,66},{65,12... | collective-permute-start | bytes 1327112 | tf_op jit(solution)/shard_map/ppermute | solution.py:27
  96.8 11.9 %collective-permute-start.15 = (bf16[2,144,768]{2,1,0:T(8,128)(2,1)S(1)}, bf16[2,144,768]{2,1,0:T(8,128)(2,1)S(1)}, u32[]{:S(2)}, u32[]{:S(2)}) collective-permute-start(bf16[2,144,768]{2,1,0:T(8,128)(2,1)S(1)} %get-tuple-element.59), channel_id=1, source_target_pairs={{0,6},{1,193},{2,0},{3,195},{4,2},{5,197},{6,4},{7,199},{64,70},{6... | collective-permute-start | bytes 1327112 | tf_op jit(solution)/shard_map/ppermute | solution.py:27
  99.6 9.9 %collective-permute-start.17 = (bf16[2,144,768]{2,1,0:T(8,128)(2,1)S(1)}, bf16[2,144,768]{2,1,0:T(8,128)(2,1)S(1)}, u32[]{:S(2)}, u32[]{:S(2)}) collective-permute-start(bf16[2,144,768]{2,1,0:T(8,128)(2,1)S(1)} %get-tuple-element.76), channel_id=1, source_target_pairs={{0,6},{1,193},{2,0},{3,195},{4,2},{5,197},{6,4},{7,199},{64,70},{6... | collective-permute-start | bytes 1327112 | tf_op jit(solution)/shard_map/ppermute | solution.py:27
  101.1 8.8 %collective-permute-start.16 = (bf16[2,144,768]{2,1,0:T(8,128)(2,1)S(1)}, bf16[2,144,768]{2,1,0:T(8,128)(2,1)S(1)}, u32[]{:S(2)}, u32[]{:S(2)}) collective-permute-start(bf16[2,144,768]{2,1,0:T(8,128)(2,1)S(1)} %get-tuple-element.77), channel_id=1, source_target_pairs={{0,2},{1,65},{2,4},{3,67},{4,6},{5,69},{6,0},{7,71},{64,66},{65,12... | collective-permute-start | bytes 1327112 | tf_op jit(solution)/shard_map/ppermute | solution.py:27
  109.9 4.5 %collective-permute-start.22 = (bf16[4,768,256]{2,1,0:T(8,128)(2,1)S(1)}, bf16[4,768,256]{2,1,0:T(8,128)(2,1)S(1)}, u32[]{:S(2)}, u32[]{:S(2)}) collective-permute-start(bf16[4,768,256]{2,1,0:T(8,128)(2,1)S(1)} %shard_map.110), channel_id=1, source_target_pairs={{0,1},{1,0},{2,3},{3,2},{4,5},{5,4},{6,7},{7,6},{8,9},{9,8},{10,11... | collective-permute-start | bytes 4718600 | tf_op jit(solution)/shard_map/ppermute | solution.py:15
  110.7 6.7 %collective-permute-start.20 = (bf16[144,768]{1,0:T(8,128)(2,1)S(1)}, bf16[144,768]{1,0:T(8,128)(2,1)S(1)}, u32[]{:S(2)}, u32[]{:S(2)}) collective-permute-start(bf16[144,768]{1,0:T(8,128)(2,1)S(1)} %get-tuple-element.82), channel_id=1, source_target_pairs={{0,128},{1,5},{2,130},{3,7},{4,132},{5,1},{6,134},{7,3},{64,192},{... | collective-permute-start | bytes 663560 | tf_op jit(solution)/shard_map/ppermute | solution.py:27
  112.0 8.4 %collective-permute-start.19 = (bf16[144,768]{1,0:T(8,128)(2,1)S(1)}, bf16[144,768]{1,0:T(8,128)(2,1)S(1)}, u32[]{:S(2)}, u32[]{:S(2)}) collective-permute-start(bf16[144,768]{1,0:T(8,128)(2,1)S(1)} %get-tuple-element.83), channel_id=1, source_target_pairs={{0,192},{1,7},{2,194},{3,1},{4,196},{5,3},{6,198},{7,5},{64,0},{65... | collective-permute-start | bytes 663560 | tf_op jit(solution)/shard_map/ppermute | solution.py:27
  113.9 18.3 %copy-start.3 = (bf16[320,128]{1,0:T(8,128)(2,1)S(1)}, bf16[320,128]{1,0:T(8,128)(2,1)}, u32[]{:S(2)}) copy-start(bf16[320,128]{1,0:T(8,128)(2,1)} %get-tuple-element.39.pick) | copy-start | bytes 245764
  113.9 6.5 %collective-permute-start.18 = (bf16[144,768]{1,0:T(8,128)(2,1)S(1)}, bf16[144,768]{1,0:T(8,128)(2,1)S(1)}, u32[]{:S(2)}, u32[]{:S(2)}) collective-permute-start(bf16[144,768]{1,0:T(8,128)(2,1)S(1)} %get-tuple-element.84), channel_id=1, source_target_pairs={{0,64},{1,3},{2,66},{3,5},{4,68},{5,7},{6,70},{7,1},{64,128},{65,6... | collective-permute-start | bytes 663560 | tf_op jit(solution)/shard_map/ppermute | solution.py:27
  132.5 4.7 %collective-permute-start.23 = (f32[128,384]{1,0:T(8,128)S(1)}, f32[128,384]{1,0:T(8,128)S(1)}, u32[]{:S(2)}, u32[]{:S(2)}) collective-permute-start(f32[128,384]{1,0:T(8,128)S(1)} %get-tuple-element.71), channel_id=1, source_target_pairs={{0,1},{1,0},{2,3},{3,2},{4,5},{5,4},{6,7},{7,6},{8,9},{9,8},{10,11... | collective-permute-start | bytes 589832 | tf_op jit(solution)/shard_map/ppermute | solution.py:15

commit v2 on v1

--- a/solution.py
+++ b/solution.py
@@ -108,9 +108,10 @@
         hit_x, hit_y = jnp.where(is_x, hit, 0.0), jnp.where(is_y, hit, 0.0)
         gate = jnp.where(first, gates[0:1, :], 0.0) + jnp.where(second, gates[1:2, :], 0.0)
         gate = jnp.sum(hit_y * gate, axis=1, keepdims=True)
-        x = dot(hit_x.astype(BF), tok[...], ((1,), (0,)))
-        y = dot(hit_y.astype(BF), grad[...], ((1,), (0,))) * gate
-        sent[...] = (x + y).astype(BF)
+        hits = jnp.concatenate([hit_x, hit_y], axis=1).astype(BF)
+        sources = jnp.concatenate([tok[...], grad[...]], axis=0)
+        scale = jnp.where(is_y, gate, 1.0)
+        sent[...] = (dot(hits, sources, ((1,), (0,))) * scale).astype(BF)
         pick[...] = (hit_x + hit_y).astype(BF)
 
     column = pl.BlockSpec((rows, cols), lambda k, xi: (0, x_of(xi)))

time: 138 us -> 138 us (level)
  no operation moved by 1% of the time
where the time goes in v2:
time: 138 us
  Pallas kernels  35.3 us (26%)
  blocking collectives  35.3 us (26%)
  starting transfers between devices  34.1 us (25%)
  waiting for transfers between devices  30.5 us (22%)
  other arithmetic  1.61 us (1%)
    all_to_all x2, blocking collectives, exchange(): a = lax.all_to_all(a, 'expert', split_axis=0, concat_axis=0, tiled=True)  35.3 us
    pallas_call x11, Pallas kernels, call_inside(): pl.pallas_call(body, in_specs=[SCALARS] + [INSIDE] * (len(args) - 1), out...  29.9 us
    ppermute x18, waiting for transfers between devices, ring(): return lax.ppermute(a, ('dp', 'x', 'core'), pairs)  29.4 us
    ppermute x18, starting transfers between devices, ring(): return lax.ppermute(a, ('dp', 'x', 'core'), pairs)  22.7 us
    ppermute x6, starting transfers between devices, swap(): return lax.ppermute(a, 'core', [(0, 1), (1, 0)])  11.4 us
    pallas_call x2, Pallas kernels, call(): pl.pallas_call(body, grid_spec=pltpu.PrefetchScalarGridSpec(num_scalar_pr...  5.38 us
  transfers between devices with their start and end apart: 24, of which 13 were waited for; matrix products, arithmetic and copies ran while one was open for 1% of the time, Pallas kernels for 22%

profile of v2, /device:TPU:1, one launch (start us, length us, event | category | flops | bytes accessed | tf_op | source)
XLA Modules:
  0.0 137.8 jit_solution(4666110478787245370)
XLA Ops:
  0.6 3.3 %collective-permute-start = (bf16[3072,256]{1,0:T(8,128)(2,1)}, bf16[3072,256]{1,0:T(8,128)(2,1)S(1)}, u32[]{:S(2)}, u32[]{:S(2)}) collective-permute-start(bf16[3072,256]{1,0:T(8,128)(2,1)} %bitcast.44), channel_id=1, source_target_pairs={{0,1},{1,0},{2,3},{3,2},{4,5},{5,4},{6,7},{7,6},{8,9},{9,8},{10,11... | collective-permute-start | bytes 4718600 | tf_op jit(solution)/shard_map/ppermute | solution.py:15
  4.1 0.4 collective-permute-start.2
  4.5 2.3 %shard_map.102 = (bf16[320,768]{1,0:T(8,128)(2,1)}, bf16[320,128]{1,0:T(8,128)(2,1)}) custom-call(s32[1]{0:T(128)} %bitcast.xi, s32[2,128]{1,0:T(2,128)} %bitcast.59, f32[2,128]{1,0:T(2,128)} %bitcast.60, bf16[128,3072]{1,0:T(8,128)(2,1)} %tok.1, bf16[128,3072]{1,0:T(8,128)(2,1)} %grad.1), custom_call_target="tpu_custom_call" | custom-call | flops 125829120 | bytes 8388608 | tf_op jit(solution)/shard_map/pallas_call | solution.py:51
  6.7 23.9 %all_to_all.10 = bf16[8,40,768]{2,1,0:T(8,128)(2,1)S(1)} all-to-all(bf16[8,40,768]{2,1,0:T(8,128)(2,1)} %bitcast.58), channel_id=1, replica_groups=mesh['dp'=4,'expert'=8,'x'=4,'core'=2] {'expert'}, dimensions={0} | all-to-all | bytes 983040 | tf_op jit(solution)/shard_map/all_to_all | solution.py:513
  30.6 0.4 shard_map.103
  31.0 1.4 collective-permute-start.6
  32.4 2.6 %collective-permute-start.5 = (bf16[288,768]{1,0:T(8,128)(2,1)S(1)}, bf16[288,768]{1,0:T(8,128)(2,1)S(1)}, u32[]{:S(2)}, u32[]{:S(2)}) collective-permute-start(bf16[288,768]{1,0:T(8,128)(2,1)S(1)} %shard_map.103), channel_id=1, source_target_pairs={{0,4},{1,129},{2,6},{3,131},{4,0},{5,133},{6,2},{7,135},{64,68},{6... | collective-permute-start | bytes 1327112 | tf_op jit(solution)/shard_map/ppermute | solution.py:27
  35.0 1.1 collective-permute-start.3
  36.1 3.7 %collective-permute-done.6 = bf16[288,768]{1,0:T(8,128)(2,1)S(1)} collective-permute-done((bf16[288,768]{1,0:T(8,128)(2,1)S(1)}, bf16[288,768]{1,0:T(8,128)(2,1)S(1)}, u32[]{:S(2)}, u32[]{:S(2)}) %collective-permute-start.6) | collective-permute-done | bytes 442400 | tf_op jit(solution)/shard_map/ppermute | solution.py:27
  39.8 5.9 %collective-permute-done.5 = bf16[288,768]{1,0:T(8,128)(2,1)S(1)} collective-permute-done((bf16[288,768]{1,0:T(8,128)(2,1)S(1)}, bf16[288,768]{1,0:T(8,128)(2,1)S(1)}, u32[]{:S(2)}, u32[]{:S(2)}) %collective-permute-start.5) | collective-permute-done | bytes 442400 | tf_op jit(solution)/shard_map/ppermute | solution.py:27
  45.8 1.0 collective-permute-start.7
  46.9 1.8 %collective-permute-start.4 = (bf16[2,288,768]{2,1,0:T(8,128)(2,1)S(1)}, bf16[2,288,768]{2,1,0:T(8,128)(2,1)S(1)}, u32[]{:S(2)}, u32[]{:S(2)}) collective-permute-start(bf16[2,288,768]{2,1,0:T(8,128)(2,1)S(1)} %pad_maximum_fusion.1), channel_id=1, source_target_pairs={{0,192},{1,7},{2,194},{3,1},{4,196},{5,3},{6,198},{7,5},{64,0},{65... | collective-permute-start | bytes 2654216 | tf_op jit(solution)/shard_map/ppermute | solution.py:27
  48.7 3.1 %shard_map.104 = (bf16[4,768,1024]{2,1,0:T(8,128)(2,1)S(1)}, bf16[4,512,768]{2,1,0:T(8,128)(2,1)S(1)}) custom-call(s32[1]{0:T(128)} %bitcast.xi, bf16[3072,256]{1,0:T(8,128)(2,1)S(1)} %bitcast.45, bf16[3072,256]{1,0:T(8,128)(2,1)S(1)} %bitcast.47, bf16[256,3072]{1,0:T(8,128)(2,1)S(1)} %bitcast.49, bf16[3072,256]{1,0:T(8,128)(2,1)S(1)} %collective-permute-done.g2, ...), custom_call_target="tpu_custom_call" | custom-call | flops 786432 | bytes 8388608 | tf_op jit(solution)/shard_map/pallas_call | solution.py:51
  51.9 1.1 collective-permute-start.8
  53.0 0.5 collective-permute-start.9
  53.6 2.9 %shard_map.105 = (f32[4,144,1024]{2,1,0:T(8,128)S(1)}, f32[4,144,512]{2,1,0:T(8,128)S(1)}) custom-call(s32[1]{0:T(128)} %bitcast.xi, bf16[4,288,768]{2,1,0:T(8,128)(2,1)S(1)} %pad_maximum_fusion.refs_0_.p0, bf16[4,768,1024]{2,1,0:T(8,128)(2,1)S(1)} %get-tuple-element.42.refs_1_.refs_4_.w, bf16[4,512,768]{2,1,0:T(8,128)(2,1)S(1)} %get-tuple-element.43.refs_2_.refs_5_.wd), custom_call_target="tpu_custom_call" | custom-call | flops 1358954496 | bytes 8388608 | tf_op jit(solution)/shard_map/pallas_call | solution.py:65
  56.5 2.8 %collective-permute-done.7.refs_3_.p3b = bf16[2,288,768]{2,1,0:T(8,128)(2,1)S(1)} collective-permute-done((bf16[2,288,768]{2,1,0:T(8,128)(2,1)S(1)}, bf16[2,288,768]{2,1,0:T(8,128)(2,1)S(1)}, u32[]{:S(2)}, u32[]{:S(2)}) %collective-permute-start.7) | collective-permute-done | bytes 884768 | tf_op jit(solution)/shard_map/ppermute | solution.py:27
  59.3 2.8 %collective-permute-start.10 = (bf16[2,288,768]{2,1,0:T(8,128)(2,1)S(1)}, bf16[2,288,768]{2,1,0:T(8,128)(2,1)S(1)}, u32[]{:S(2)}, u32[]{:S(2)}) collective-permute-start(bf16[2,288,768]{2,1,0:T(8,128)(2,1)S(1)} %collective-permute-done.4.refs_0_.p1a), channel_id=1, source_target_pairs={{0,192},{1,7},{2,194},{3,1},{4,196},{5,3},{6,198},{7,5},{64,0},{65... | collective-permute-start | bytes 2654216 | tf_op jit(solution)/shard_map/ppermute | solution.py:27
  62.1 6.5 %collective-permute-done.8.refs_1_.p1b = bf16[2,288,768]{2,1,0:T(8,128)(2,1)S(1)} collective-permute-done((bf16[2,288,768]{2,1,0:T(8,128)(2,1)S(1)}, bf16[2,288,768]{2,1,0:T(8,128)(2,1)S(1)}, u32[]{:S(2)}, u32[]{:S(2)}) %collective-permute-start.8) | collective-permute-done | bytes 884768 | tf_op jit(solution)/shard_map/ppermute | solution.py:27
  68.8 4.5 %shard_map.106 = (f32[4,144,1024]{2,1,0:T(8,128)S(1)}, f32[4,144,512]{2,1,0:T(8,128)S(1)}) custom-call(s32[1]{0:T(128)} %bitcast.xi, bf16[2,288,768]{2,1,0:T(8,128)(2,1)S(1)} %collective-permute-done.4.refs_0_.p1a, bf16[2,288,768]{2,1,0:T(8,128)(2,1)S(1)} %collective-permute-done.8.refs_1_.p1b, bf16[2,288,768]{2,1,0:T(8,128)(2,1)S(1)} %collective-permute-done.9.refs_2_.p3a, ...), custom_call_target="tpu_custom_call" | custom-call | flops 2717908992 | bytes 8388608 | tf_op jit(solution)/shard_map/pallas_call | solution.py:65
  73.3 4.8 %collective-permute-done.10.pa.p2a = bf16[2,288,768]{2,1,0:T(8,128)(2,1)S(1)} collective-permute-done((bf16[2,288,768]{2,1,0:T(8,128)(2,1)S(1)}, bf16[2,288,768]{2,1,0:T(8,128)(2,1)S(1)}, u32[]{:S(2)}, u32[]{:S(2)}) %collective-permute-start.10) | collective-permute-done | bytes 884768 | tf_op jit(solution)/shard_map/ppermute | solution.py:27
  78.3 4.1 %shard_map.107 = (bf16[576,512]{1,0:T(8,128)(2,1)S(1)}, bf16[576,1024]{1,0:T(8,128)(2,1)S(1)}, bf16[4,144,768]{2,1,0:T(8,128)(2,1)S(1)}) custom-call(s32[1]{0:T(128)} %bitcast.xi, f32[4,144,1024]{2,1,0:T(8,128)S(1)} %get-tuple-element.48.hu, f32[4,144,512]{2,1,0:T(8,128)S(1)} %get-tuple-element.49.ga, ...), custom_call_target="tpu_custom_call" | custom-call | flops 1811939328 | bytes 8388608 | tf_op jit(solution)/shard_map/pallas_call | solution.py:65
  82.4 1.0 collective-permute-start.13
  83.5 0.5 collective-permute-start.12
  83.9 3.6 %shard_map.108 = bf16[4,768,512]{2,1,0:T(8,128)(2,1)S(1)} custom-call(s32[1]{0:T(128)} %bitcast.xi, bf16[4,288,768]{2,1,0:T(8,128)(2,1)S(1)} %pad_maximum_fusion.refs_0_.p0, bf16[2,288,768]{2,1,0:T(8,128)(2,1)S(1)} %collective-permute-done.4.refs_0_.p1a, bf16[2,288,768]{2,1,0:T(8,128)(2,1)S(1)} %collective-permute-done.8.refs_1_.p1b, ...), custom_call_target="tpu_custom_call" | custom-call | flops 1811939328 | bytes 8388608 | tf_op jit(solution)/shard_map/pallas_call | solution.py:65
  87.5 3.9 %shard_map.109 = bf16[3,4,144,768]{3,2,1,0:T(8,128)(2,1)S(1)} custom-call(s32[1]{0:T(128)} %bitcast.xi, bf16[576,1024]{1,0:T(8,128)(2,1)S(1)} %get-tuple-element.54.g, bf16[4,768,1024]{2,1,0:T(8,128)(2,1)S(1)} %get-tuple-element.42.refs_1_.refs_4_.w), custom_call_target="tpu_custom_call" | custom-call | flops 2717908992 | bytes 8388608 | tf_op jit(solution)/shard_map/pallas_call | solution.py:65
  91.4 0.7 collective-permute-done.12
  92.1 3.6 %collective-permute-start.21 = (bf16[4,768,512]{2,1,0:T(8,128)(2,1)S(1)}, bf16[4,768,512]{2,1,0:T(8,128)(2,1)S(1)}, u32[]{:S(2)}, u32[]{:S(2)}) collective-permute-start(bf16[4,768,512]{2,1,0:T(8,128)(2,1)S(1)} %shard_map.108), channel_id=1, source_target_pairs={{0,1},{1,0},{2,3},{3,2},{4,5},{5,4},{6,7},{7,6},{8,9},{9,8},{10,11... | collective-permute-start | bytes 9437192 | tf_op jit(solution)/shard_map/ppermute | solution.py:15
  95.9 0.8 collective-permute-start.14
  96.7 2.7 %collective-permute-start.15 = (bf16[2,144,768]{2,1,0:T(8,128)(2,1)S(1)}, bf16[2,144,768]{2,1,0:T(8,128)(2,1)S(1)}, u32[]{:S(2)}, u32[]{:S(2)}) collective-permute-start(bf16[2,144,768]{2,1,0:T(8,128)(2,1)S(1)} %get-tuple-element.59), channel_id=1, source_target_pairs={{0,6},{1,193},{2,0},{3,195},{4,2},{5,197},{6,4},{7,199},{64,70},{6... | collective-permute-start | bytes 1327112 | tf_op jit(solution)/shard_map/ppermute | solution.py:27
  99.5 1.5 %collective-permute-start.17 = (bf16[2,144,768]{2,1,0:T(8,128)(2,1)S(1)}, bf16[2,144,768]{2,1,0:T(8,128)(2,1)S(1)}, u32[]{:S(2)}, u32[]{:S(2)}) collective-permute-start(bf16[2,144,768]{2,1,0:T(8,128)(2,1)S(1)} %get-tuple-element.76), channel_id=1, source_target_pairs={{0,6},{1,193},{2,0},{3,195},{4,2},{5,197},{6,4},{7,199},{64,70},{6... | collective-permute-start | bytes 1327112 | tf_op jit(solution)/shard_map/ppermute | solution.py:27
  101.1 2.4 %shard_map.110 = bf16[4,768,256]{2,1,0:T(8,128)(2,1)S(1)} custom-call(s32[1]{0:T(128)} %bitcast.xi, bf16[4,288,768]{2,1,0:T(8,128)(2,1)S(1)} %pad_maximum_fusion.refs_0_.p0, bf16[2,288,768]{2,1,0:T(8,128)(2,1)S(1)} %collective-permute-done.4.refs_0_.p1a, bf16[2,288,768]{2,1,0:T(8,128)(2,1)S(1)} %collective-permute-done.8.refs_1_.p1b, ...), custom_call_target="tpu_custom_call" | custom-call | flops 905969664 | bytes 8388608 | tf_op jit(solution)/shard_map/pallas_call | solution.py:65
  103.5 5.2 %shard_map.111.mine = f32[4,768,768]{2,1,0:T(8,128)S(1)} custom-call(s32[1]{0:T(128)} %bitcast.xi, bf16[4,288,768]{2,1,0:T(8,128)(2,1)S(1)} %pad_maximum_fusion.refs_0_.p0, bf16[2,288,768]{2,1,0:T(8,128)(2,1)S(1)} %collective-permute-done.4.refs_0_.p1a, bf16[2,288,768]{2,1,0:T(8,128)(2,1)S(1)} %collective-permute-done.8.refs_1_.p1b, ...), custom_call_target="tpu_custom_call" | custom-call | flops 2717908992 | bytes 8388608 | tf_op jit(solution)/shard_map/pallas_call | solution.py:65
  108.7 0.8 collective-permute-done.17
  109.5 0.4 collective-permute-done.16
  109.8 0.4 collective-permute-start.22
  110.2 0.3 fusion.1
  110.6 1.3 collective-permute-start.20
  111.9 1.9 %collective-permute-start.19 = (bf16[144,768]{1,0:T(8,128)(2,1)S(1)}, bf16[144,768]{1,0:T(8,128)(2,1)S(1)}, u32[]{:S(2)}, u32[]{:S(2)}) collective-permute-start(bf16[144,768]{1,0:T(8,128)(2,1)S(1)} %get-tuple-element.83), channel_id=1, source_target_pairs={{0,192},{1,7},{2,194},{3,1},{4,196},{5,3},{6,198},{7,5},{64,0},{65... | collective-permute-start | bytes 663560 | tf_op jit(solution)/shard_map/ppermute | solution.py:27
  113.8 0.6 collective-permute-start.18
  114.4 2.3 %shard_map.112 = (bf16[3072,256]{1,0:T(8,128)(2,1)}, bf16[3072,256]{1,0:T(8,128)(2,1)}, bf16[256,3072]{1,0:T(8,128)(2,1)}) custom-call(s32[1]{0:T(128)} %bitcast.xi, f32[4,768,768]{2,1,0:T(8,128)S(1)} %shard_map.111.mine, bf16[4,768,512]{2,1,0:T(8,128)(2,1)S(1)} %collective-permute-done.21.up, bf16[4,768,256]{2,1,0:T(8,128)(2,1)S(1)} %collective-permute-done.22.down), custom_call_target="tpu_custom_call" | custom-call | flops 9437184 | bytes 8388608 | tf_op jit(solution)/shard_map/pallas_call | solution.py:65
  116.7 0.6 collective-permute-done.20.refs_3_
  117.3 3.0 %collective-permute-done.19.refs_2_ = bf16[144,768]{1,0:T(8,128)(2,1)S(1)} collective-permute-done((bf16[144,768]{1,0:T(8,128)(2,1)S(1)}, bf16[144,768]{1,0:T(8,128)(2,1)S(1)}, u32[]{:S(2)}, u32[]{:S(2)}) %collective-permute-start.19) | collective-permute-done | bytes 221216 | tf_op jit(solution)/shard_map/ppermute | solution.py:27
  120.3 0.4 shard_map.113
  120.7 11.4 %all_to_all.11 = bf16[8,40,384]{2,1,0:T(8,128)(2,1)S(1)} all-to-all(bf16[8,40,384]{2,1,0:T(8,128)(2,1)S(1)} %bitcast.51), channel_id=1, replica_groups=mesh['dp'=4,'expert'=8,'x'=4,'core'=2] {'expert'}, dimensions={0} | all-to-all | bytes 491520 | tf_op jit(solution)/shard_map/all_to_all | solution.py:513
  132.4 3.6 %collective-permute-start.23 = (f32[128,384]{1,0:T(8,128)S(1)}, f32[128,384]{1,0:T(8,128)S(1)}, u32[]{:S(2)}, u32[]{:S(2)}) collective-permute-start(f32[128,384]{1,0:T(8,128)S(1)} %get-tuple-element.71), channel_id=1, source_target_pairs={{0,1},{1,0},{2,3},{3,2},{4,5},{5,4},{6,7},{7,6},{8,9},{9,8},{10,11... | collective-permute-start | bytes 589832 | tf_op jit(solution)/shard_map/ppermute | solution.py:15
  136.1 1.1 collective-permute-done.23
  137.1 0.7 add_convert_fusion
  (33 shorter events, 1.6 us)
Async XLA Ops:
  0.6 30.0 %collective-permute-start = (bf16[3072,256]{1,0:T(8,128)(2,1)}, bf16[3072,256]{1,0:T(8,128)(2,1)S(1)}, u32[]{:S(2)}, u32[]{:S(2)}) collective-permute-start(bf16[3072,256]{1,0:T(8,128)(2,1)} %bitcast.44), channel_id=1, source_target_pairs={{0,1},{1,0},{2,3},{3,2},{4,5},{5,4},{6,7},{7,6},{8,9},{9,8},{10,11... | collective-permute-start | bytes 4718600 | tf_op jit(solution)/shard_map/ppermute | solution.py:15
  4.0 26.6 %collective-permute-start.1 = (bf16[3072,256]{1,0:T(8,128)(2,1)}, bf16[3072,256]{1,0:T(8,128)(2,1)S(1)}, u32[]{:S(2)}, u32[]{:S(2)}) collective-permute-start(bf16[3072,256]{1,0:T(8,128)(2,1)} %bitcast.46), channel_id=1, source_target_pairs={{0,1},{1,0},{2,3},{3,2},{4,5},{5,4},{6,7},{7,6},{8,9},{9,8},{10,11... | collective-permute-start | bytes 4718600 | tf_op jit(solution)/shard_map/ppermute | solution.py:15
  4.1 26.6 %collective-permute-start.2 = (bf16[256,3072]{1,0:T(8,128)(2,1)}, bf16[256,3072]{1,0:T(8,128)(2,1)}, u32[]{:S(2)}, u32[]{:S(2)}) collective-permute-start(bf16[256,3072]{1,0:T(8,128)(2,1)} %bitcast.48), channel_id=1, source_target_pairs={{0,1},{1,0},{2,3},{3,2},{4,5},{5,4},{6,7},{7,6},{8,9},{9,8},{10,11... | collective-permute-start | bytes 4718600 | tf_op jit(solution)/shard_map/ppermute | solution.py:15
  6.7 42.0 %copy-start.2 = (bf16[1,256,3072]{2,1,0:T(8,128)(2,1)S(1)}, bf16[1,256,3072]{2,1,0:T(8,128)(2,1)}, u32[]{:S(2)}) copy-start(bf16[1,256,3072]{2,1,0:T(8,128)(2,1)} %param.13) | copy-start | bytes 4718596
  31.0 8.8 %collective-permute-start.6 = (bf16[288,768]{1,0:T(8,128)(2,1)S(1)}, bf16[288,768]{1,0:T(8,128)(2,1)S(1)}, u32[]{:S(2)}, u32[]{:S(2)}) collective-permute-start(bf16[288,768]{1,0:T(8,128)(2,1)S(1)} %shard_map.103), channel_id=1, source_target_pairs={{0,2},{1,65},{2,4},{3,67},{4,6},{5,69},{6,0},{7,71},{64,66},{65,12... | collective-permute-start | bytes 1327112 | tf_op jit(solution)/shard_map/ppermute | solution.py:27
  32.4 13.3 %collective-permute-start.5 = (bf16[288,768]{1,0:T(8,128)(2,1)S(1)}, bf16[288,768]{1,0:T(8,128)(2,1)S(1)}, u32[]{:S(2)}, u32[]{:S(2)}) collective-permute-start(bf16[288,768]{1,0:T(8,128)(2,1)S(1)} %shard_map.103), channel_id=1, source_target_pairs={{0,4},{1,129},{2,6},{3,131},{4,0},{5,133},{6,2},{7,135},{64,68},{6... | collective-permute-start | bytes 1327112 | tf_op jit(solution)/shard_map/ppermute | solution.py:27
  35.0 11.8 %collective-permute-start.3 = (bf16[288,768]{1,0:T(8,128)(2,1)S(1)}, bf16[288,768]{1,0:T(8,128)(2,1)S(1)}, u32[]{:S(2)}, u32[]{:S(2)}) collective-permute-start(bf16[288,768]{1,0:T(8,128)(2,1)S(1)} %shard_map.103), channel_id=1, source_target_pairs={{0,6},{1,193},{2,0},{3,195},{4,2},{5,197},{6,4},{7,199},{64,70},{6... | collective-permute-start | bytes 1327112 | tf_op jit(solution)/shard_map/ppermute | solution.py:27
  45.7 3.0 %copy-start = (bf16[1,3072,256]{2,1,0:T(8,128)(2,1)S(1)}, bf16[1,3072,256]{2,1,0:T(8,128)(2,1)}, u32[]{:S(2)}) copy-start(bf16[1,3072,256]{2,1,0:T(8,128)(2,1)} %param.11) | copy-start | bytes 4718596
  45.7 3.0 %copy-start.1 = (bf16[1,3072,256]{2,1,0:T(8,128)(2,1)S(1)}, bf16[1,3072,256]{2,1,0:T(8,128)(2,1)}, u32[]{:S(2)}) copy-start(bf16[1,3072,256]{2,1,0:T(8,128)(2,1)} %param.12) | copy-start | bytes 4718596
  45.8 13.5 %collective-permute-start.7 = (bf16[2,288,768]{2,1,0:T(8,128)(2,1)S(1)}, bf16[2,288,768]{2,1,0:T(8,128)(2,1)S(1)}, u32[]{:S(2)}, u32[]{:S(2)}) collective-permute-start(bf16[2,288,768]{2,1,0:T(8,128)(2,1)S(1)} %pad_maximum_fusion.2), channel_id=1, source_target_pairs={{0,64},{1,3},{2,66},{3,5},{4,68},{5,7},{6,70},{7,1},{64,128},{65,6... | collective-permute-start | bytes 2654216 | tf_op jit(solution)/shard_map/ppermute | solution.py:27
  46.9 12.4 %collective-permute-start.4 = (bf16[2,288,768]{2,1,0:T(8,128)(2,1)S(1)}, bf16[2,288,768]{2,1,0:T(8,128)(2,1)S(1)}, u32[]{:S(2)}, u32[]{:S(2)}) collective-permute-start(bf16[2,288,768]{2,1,0:T(8,128)(2,1)S(1)} %pad_maximum_fusion.1), channel_id=1, source_target_pairs={{0,192},{1,7},{2,194},{3,1},{4,196},{5,3},{6,198},{7,5},{64,0},{65... | collective-permute-start | bytes 2654216 | tf_op jit(solution)/shard_map/ppermute | solution.py:27
  51.9 16.8 %collective-permute-start.8 = (bf16[2,288,768]{2,1,0:T(8,128)(2,1)S(1)}, bf16[2,288,768]{2,1,0:T(8,128)(2,1)S(1)}, u32[]{:S(2)}, u32[]{:S(2)}) collective-permute-start(bf16[2,288,768]{2,1,0:T(8,128)(2,1)S(1)} %pad_maximum_fusion.2), channel_id=1, source_target_pairs={{0,192},{1,7},{2,194},{3,1},{4,196},{5,3},{6,198},{7,5},{64,0},{65... | collective-permute-start | bytes 2654216 | tf_op jit(solution)/shard_map/ppermute | solution.py:27
  53.0 15.8 %collective-permute-start.9 = (bf16[2,288,768]{2,1,0:T(8,128)(2,1)S(1)}, bf16[2,288,768]{2,1,0:T(8,128)(2,1)S(1)}, u32[]{:S(2)}, u32[]{:S(2)}) collective-permute-start(bf16[2,288,768]{2,1,0:T(8,128)(2,1)S(1)} %pad_maximum_fusion.1), channel_id=1, source_target_pairs={{0,64},{1,3},{2,66},{3,5},{4,68},{5,7},{6,70},{7,1},{64,128},{65,6... | collective-permute-start | bytes 2654216 | tf_op jit(solution)/shard_map/ppermute | solution.py:27
  59.3 18.8 %collective-permute-start.10 = (bf16[2,288,768]{2,1,0:T(8,128)(2,1)S(1)}, bf16[2,288,768]{2,1,0:T(8,128)(2,1)S(1)}, u32[]{:S(2)}, u32[]{:S(2)}) collective-permute-start(bf16[2,288,768]{2,1,0:T(8,128)(2,1)S(1)} %collective-permute-done.4.refs_0_.p1a), channel_id=1, source_target_pairs={{0,192},{1,7},{2,194},{3,1},{4,196},{5,3},{6,198},{7,5},{64,0},{65... | collective-permute-start | bytes 2654216 | tf_op jit(solution)/shard_map/ppermute | solution.py:27
  62.1 16.1 %collective-permute-start.11 = (bf16[2,288,768]{2,1,0:T(8,128)(2,1)S(1)}, bf16[2,288,768]{2,1,0:T(8,128)(2,1)S(1)}, u32[]{:S(2)}, u32[]{:S(2)}) collective-permute-start(bf16[2,288,768]{2,1,0:T(8,128)(2,1)S(1)} %collective-permute-done.7.refs_3_.p3b), channel_id=1, source_target_pairs={{0,64},{1,3},{2,66},{3,5},{4,68},{5,7},{6,70},{7,1},{64,128},{65,6... | collective-permute-start | bytes 2654216 | tf_op jit(solution)/shard_map/ppermute | solution.py:27
  82.4 9.0 %collective-permute-start.13 = (bf16[2,144,768]{2,1,0:T(8,128)(2,1)S(1)}, bf16[2,144,768]{2,1,0:T(8,128)(2,1)S(1)}, u32[]{:S(2)}, u32[]{:S(2)}) collective-permute-start(bf16[2,144,768]{2,1,0:T(8,128)(2,1)S(1)} %get-tuple-element.80), channel_id=1, source_target_pairs={{0,6},{1,193},{2,0},{3,195},{4,2},{5,197},{6,4},{7,199},{64,70},{6... | collective-permute-start | bytes 1327112 | tf_op jit(solution)/shard_map/ppermute | solution.py:27
  83.5 8.7 %collective-permute-start.12 = (bf16[2,144,768]{2,1,0:T(8,128)(2,1)S(1)}, bf16[2,144,768]{2,1,0:T(8,128)(2,1)S(1)}, u32[]{:S(2)}, u32[]{:S(2)}) collective-permute-start(bf16[2,144,768]{2,1,0:T(8,128)(2,1)S(1)} %get-tuple-element.81), channel_id=1, source_target_pairs={{0,2},{1,65},{2,4},{3,67},{4,6},{5,69},{6,0},{7,71},{64,66},{65,12... | collective-permute-start | bytes 1327112 | tf_op jit(solution)/shard_map/ppermute | solution.py:27
  92.1 22.3 %collective-permute-start.21 = (bf16[4,768,512]{2,1,0:T(8,128)(2,1)S(1)}, bf16[4,768,512]{2,1,0:T(8,128)(2,1)S(1)}, u32[]{:S(2)}, u32[]{:S(2)}) collective-permute-start(bf16[4,768,512]{2,1,0:T(8,128)(2,1)S(1)} %shard_map.108), channel_id=1, source_target_pairs={{0,1},{1,0},{2,3},{3,2},{4,5},{5,4},{6,7},{7,6},{8,9},{9,8},{10,11... | collective-permute-start | bytes 9437192 | tf_op jit(solution)/shard_map/ppermute | solution.py:15
  95.9 12.8 %collective-permute-start.14 = (bf16[2,144,768]{2,1,0:T(8,128)(2,1)S(1)}, bf16[2,144,768]{2,1,0:T(8,128)(2,1)S(1)}, u32[]{:S(2)}, u32[]{:S(2)}) collective-permute-start(bf16[2,144,768]{2,1,0:T(8,128)(2,1)S(1)} %get-tuple-element.58), channel_id=1, source_target_pairs={{0,2},{1,65},{2,4},{3,67},{4,6},{5,69},{6,0},{7,71},{64,66},{65,12... | collective-permute-start | bytes 1327112 | tf_op jit(solution)/shard_map/ppermute | solution.py:27
  96.7 11.9 %collective-permute-start.15 = (bf16[2,144,768]{2,1,0:T(8,128)(2,1)S(1)}, bf16[2,144,768]{2,1,0:T(8,128)(2,1)S(1)}, u32[]{:S(2)}, u32[]{:S(2)}) collective-permute-start(bf16[2,144,768]{2,1,0:T(8,128)(2,1)S(1)} %get-tuple-element.59), channel_id=1, source_target_pairs={{0,6},{1,193},{2,0},{3,195},{4,2},{5,197},{6,4},{7,199},{64,70},{6... | collective-permute-start | bytes 1327112 | tf_op jit(solution)/shard_map/ppermute | solution.py:27
  99.5 9.9 %collective-permute-start.17 = (bf16[2,144,768]{2,1,0:T(8,128)(2,1)S(1)}, bf16[2,144,768]{2,1,0:T(8,128)(2,1)S(1)}, u32[]{:S(2)}, u32[]{:S(2)}) collective-permute-start(bf16[2,144,768]{2,1,0:T(8,128)(2,1)S(1)} %get-tuple-element.76), channel_id=1, source_target_pairs={{0,6},{1,193},{2,0},{3,195},{4,2},{5,197},{6,4},{7,199},{64,70},{6... | collective-permute-start | bytes 1327112 | tf_op jit(solution)/shard_map/ppermute | solution.py:27
  101.0 8.8 %collective-permute-start.16 = (bf16[2,144,768]{2,1,0:T(8,128)(2,1)S(1)}, bf16[2,144,768]{2,1,0:T(8,128)(2,1)S(1)}, u32[]{:S(2)}, u32[]{:S(2)}) collective-permute-start(bf16[2,144,768]{2,1,0:T(8,128)(2,1)S(1)} %get-tuple-element.77), channel_id=1, source_target_pairs={{0,2},{1,65},{2,4},{3,67},{4,6},{5,69},{6,0},{7,71},{64,66},{65,12... | collective-permute-start | bytes 1327112 | tf_op jit(solution)/shard_map/ppermute | solution.py:27
  109.8 4.5 %collective-permute-start.22 = (bf16[4,768,256]{2,1,0:T(8,128)(2,1)S(1)}, bf16[4,768,256]{2,1,0:T(8,128)(2,1)S(1)}, u32[]{:S(2)}, u32[]{:S(2)}) collective-permute-start(bf16[4,768,256]{2,1,0:T(8,128)(2,1)S(1)} %shard_map.110), channel_id=1, source_target_pairs={{0,1},{1,0},{2,3},{3,2},{4,5},{5,4},{6,7},{7,6},{8,9},{9,8},{10,11... | collective-permute-start | bytes 4718600 | tf_op jit(solution)/shard_map/ppermute | solution.py:15
  110.6 6.7 %collective-permute-start.20 = (bf16[144,768]{1,0:T(8,128)(2,1)S(1)}, bf16[144,768]{1,0:T(8,128)(2,1)S(1)}, u32[]{:S(2)}, u32[]{:S(2)}) collective-permute-start(bf16[144,768]{1,0:T(8,128)(2,1)S(1)} %get-tuple-element.82), channel_id=1, source_target_pairs={{0,128},{1,5},{2,130},{3,7},{4,132},{5,1},{6,134},{7,3},{64,192},{... | collective-permute-start | bytes 663560 | tf_op jit(solution)/shard_map/ppermute | solution.py:27
  111.9 8.4 %collective-permute-start.19 = (bf16[144,768]{1,0:T(8,128)(2,1)S(1)}, bf16[144,768]{1,0:T(8,128)(2,1)S(1)}, u32[]{:S(2)}, u32[]{:S(2)}) collective-permute-start(bf16[144,768]{1,0:T(8,128)(2,1)S(1)} %get-tuple-element.83), channel_id=1, source_target_pairs={{0,192},{1,7},{2,194},{3,1},{4,196},{5,3},{6,198},{7,5},{64,0},{65... | collective-permute-start | bytes 663560 | tf_op jit(solution)/shard_map/ppermute | solution.py:27
  113.8 18.3 %copy-start.3 = (bf16[320,128]{1,0:T(8,128)(2,1)S(1)}, bf16[320,128]{1,0:T(8,128)(2,1)}, u32[]{:S(2)}) copy-start(bf16[320,128]{1,0:T(8,128)(2,1)} %get-tuple-element.39.pick) | copy-start | bytes 245764
  113.8 6.5 %collective-permute-start.18 = (bf16[144,768]{1,0:T(8,128)(2,1)S(1)}, bf16[144,768]{1,0:T(8,128)(2,1)S(1)}, u32[]{:S(2)}, u32[]{:S(2)}) collective-permute-start(bf16[144,768]{1,0:T(8,128)(2,1)S(1)} %get-tuple-element.84), channel_id=1, source_target_pairs={{0,64},{1,3},{2,66},{3,5},{4,68},{5,7},{6,70},{7,1},{64,128},{65,6... | collective-permute-start | bytes 663560 | tf_op jit(solution)/shard_map/ppermute | solution.py:27
  132.4 4.7 %collective-permute-start.23 = (f32[128,384]{1,0:T(8,128)S(1)}, f32[128,384]{1,0:T(8,128)S(1)}, u32[]{:S(2)}, u32[]{:S(2)}) collective-permute-start(f32[128,384]{1,0:T(8,128)S(1)} %get-tuple-element.71), channel_id=1, source_target_pairs={{0,1},{1,0},{2,3},{3,2},{4,5},{5,4},{6,7},{7,6},{8,9},{9,8},{10,11... | collective-permute-start | bytes 589832 | tf_op jit(solution)/shard_map/ppermute | solution.py:15
